TPU v7x, 32 devices: a whole 2x2x4 slice. The times are simulated.
32 devices in a mesh: dp: 2 (over x), row: 4 (over y, core), col: 4 (over z).
Axes of the slice: x: 2, y: 2, z: 4, core: 2. Of those that a mesh axis runs over, the one named last changes fastest.
Arguments:
- tokens: bfloat16 [768, 16384], P('col', ('dp', 'row')), may hold values from -6 to 6
- segments: int32 [8, 2048], P('dp'), may hold values from 0 to 7, never falling along the last dimension, each value on 1 to 819 neighbouring positions
- ln1_gain: bfloat16 [768], P('col'), may hold values from 0.3984375 to 1.59375
- ln1_bias: bfloat16 [768], P('col'), may hold values from -1.75 to 1.75
- w_query: bfloat16 [768, 768], P('col', 'row'), may hold values from -0.21875 to 0.21875
- q_bias: bfloat16 [768], P('row'), may hold values from -1.75 to 1.75
- w_key: bfloat16 [768, 768], P('col', 'row'), may hold values from -0.21875 to 0.21875
- w_value: bfloat16 [768, 768], P('col', 'row'), may hold values from -0.21875 to 0.21875
- v_bias: bfloat16 [768], P('row'), may hold values from -1.75 to 1.75
- w_out: bfloat16 [768, 768], P('row', 'col'), may hold values from -1.75 to 1.75
- out_bias: bfloat16 [768], P('col'), may hold values from -1.75 to 1.75
- ln2_gain: bfloat16 [768], P('col'), may hold values from 0.3984375 to 1.59375
- ln2_bias: bfloat16 [768], P('col'), may hold values from -1.75 to 1.75
- w_up: bfloat16 [768, 3072], P('col', 'row'), may hold values from -0.21875 to 0.21875
- up_bias: bfloat16 [3072], P('row'), may hold values from -1.75 to 1.75
- w_down: bfloat16 [768, 3072], P('col', 'row'), may hold values from -0.109375 to 0.109375
- down_bias: bfloat16 [768], P('col'), may hold values from -1.75 to 1.75
- cotangent: bfloat16 [768, 16384], P('col', ('dp', 'row')), may hold values from -6 to 6
Outputs:
- out: bfloat16 [768, 16384], P('col', ('dp', 'row'))
- grad_tokens: float32 [768, 16384], P('col', ('dp', 'row'))
- grad_ln1_gain: float32 [768], P('col')
- grad_ln1_bias: float32 [768], P('col')
- grad_w_query: float32 [768, 768], P('col', 'row')
- grad_q_bias: float32 [768], P('row')
- grad_w_key: float32 [768, 768], P('col', 'row')
- grad_w_value: float32 [768, 768], P('col', 'row')
- grad_v_bias: float32 [768], P('row')
- grad_w_out: float32 [768, 768], P('row', 'col')
- grad_out_bias: float32 [768], P('col')
- grad_ln2_gain: float32 [768], P('col')
- grad_ln2_bias: float32 [768], P('col')
- grad_w_up: float32 [768, 3072], P('col', 'row')
- grad_up_bias: float32 [3072], P('row')
- grad_w_down: float32 [768, 3072], P('col', 'row')
- grad_down_bias: float32 [768], P('col')
Inputs may be any that keep to these rules, and one draw needn't show every extreme that they name: `segments`: numbers never fall along a sequence and start at 0; a document has at most 819 tokens.
All inputs are finite; a program needn't handle non-finite values.
Results may differ from a plain program's by a relative error of at most 0.013.
Values may be sent and summed in bfloat16 or wider, within the bound.
A program may use at most 384 MiB of HBM per device.

v0:
```python
import jax
import jax.numpy as jnp
from jax import lax
from jax.sharding import PartitionSpec as P

HD = 64


EPS = 1e-05
NEG = -1000000000.0


def col_totals(first_sum, second_sum):
    return lax.psum((first_sum, second_sum), "col")


def gather_rows(activation):
    return lax.all_gather(activation, "row", axis=0, tiled=True)


def gather_columns(activation):
    return lax.all_gather(activation, "col", axis=0, tiled=True)


def product_columns(gathered, weight):
    own_rows = gathered.shape[0] // lax.axis_size("col")

    def partial_term(row_start, row_count):
        return jnp.dot(gathered, weight, preferred_element_type=jnp.float32)

    return lax.psum_scatter(
        partial_term(jnp.int32(0), own_rows * lax.axis_size("col")),
        "col",
        scatter_dimension=0,
        tiled=True,
    )


def product_rows(gathered, weight):
    own_rows = gathered.shape[0] // lax.axis_size("row")

    def partial_term(row_start, row_count):
        return jnp.dot(gathered, weight, preferred_element_type=jnp.float32)

    return lax.psum_scatter(
        partial_term(jnp.int32(0), own_rows * lax.axis_size("row")),
        "row",
        scatter_dimension=0,
        tiled=True,
    )


def norm_forward(values, norm_gain, norm_shift):
    feature_count = values.shape[1] * lax.axis_size("col")
    totals, squares = col_totals(jnp.sum(values, 1), jnp.sum(values * values, 1))
    center = totals / feature_count
    spread = squares / feature_count - center * center
    inverse = lax.rsqrt(spread + EPS)
    normed = (values - center[:, None]) * inverse[:, None]
    return ((normed * norm_gain + norm_shift).astype(jnp.bfloat16), normed, inverse)


def norm_backward(incoming, normed, inverse, norm_gain):
    feature_count = normed.shape[1] * lax.axis_size("col")
    scaled = incoming * norm_gain
    first_sum, second_sum = col_totals(jnp.sum(scaled, 1), jnp.sum(scaled * normed, 1))
    return inverse[:, None] * (
        scaled - first_sum[:, None] / feature_count - normed * (second_sum[:, None] / feature_count)
    )


def sequence_parts(flat_rows, sequences):
    return flat_rows.reshape(sequences, -1, flat_rows.shape[1] // HD, HD)


def block_scores(query_block, key_rows, row_start, block_rows, labels):
    places = jnp.arange(labels.shape[0], dtype=jnp.int32)
    query_places = row_start + jnp.arange(block_rows, dtype=jnp.int32)
    query_labels = lax.dynamic_slice_in_dim(labels, row_start, block_rows, 0)
    allowed = (query_places[:, None] >= places[None, :]) & (
        query_labels[:, None] == labels[None, :]
    )
    scores = jnp.einsum(
        "qhd,khd->hqk", query_block, key_rows, preferred_element_type=jnp.float32
    ) * HD ** (-0.5)
    return jnp.where(allowed[None], scores, NEG)


def attend_forward(query_flat, key_flat, value_flat, segments):
    sequences, length = segments.shape
    block_rows = min(512, length)
    per_sequence = length // block_rows
    query_all = sequence_parts(query_flat, sequences)
    key_all = sequence_parts(key_flat, sequences)
    value_all = sequence_parts(value_flat, sequences)

    def attend_one_block(number):
        sequence = number // per_sequence
        row_start = number % per_sequence * block_rows
        labels = lax.dynamic_index_in_dim(segments, sequence, 0, keepdims=False)
        key_rows = lax.dynamic_index_in_dim(key_all, sequence, 0, keepdims=False)
        value_rows = lax.dynamic_index_in_dim(value_all, sequence, 0, keepdims=False)
        query_seq = lax.dynamic_index_in_dim(query_all, sequence, 0, keepdims=False)
        query_block = lax.dynamic_slice_in_dim(query_seq, row_start, block_rows, 0)
        scores = block_scores(query_block, key_rows, row_start, block_rows, labels)
        highest = jnp.max(scores, -1, keepdims=True)
        weights = jnp.exp(scores - highest)
        totals = jnp.sum(weights, -1, keepdims=True)
        probability = (weights / totals).astype(jnp.bfloat16)
        attended = jnp.einsum(
            "hqk,khd->qhd", probability, value_rows, preferred_element_type=jnp.float32
        )
        return (attended.astype(jnp.bfloat16), (highest + jnp.log(totals))[..., 0])

    attended, log_totals = lax.map(
        attend_one_block, jnp.arange(sequences * per_sequence, dtype=jnp.int32)
    )
    return (attended.reshape(query_flat.shape), log_totals)


def attend_backward(query_flat, key_flat, value_flat, grad_flat, log_totals, segments):
    sequences, length = segments.shape
    block_rows = min(512, length)
    per_sequence = length // block_rows
    query_all = sequence_parts(query_flat, sequences)
    key_all = sequence_parts(key_flat, sequences)
    value_all = sequence_parts(value_flat, sequences)
    grad_all = sequence_parts(grad_flat, sequences)
    stats_all = log_totals.reshape(sequences, per_sequence, log_totals.shape[1], block_rows)

    def one_sequence(sequence):
        labels = lax.dynamic_index_in_dim(segments, sequence, 0, keepdims=False)
        query_seq = lax.dynamic_index_in_dim(query_all, sequence, 0, keepdims=False)
        key_rows = lax.dynamic_index_in_dim(key_all, sequence, 0, keepdims=False)
        value_rows = lax.dynamic_index_in_dim(value_all, sequence, 0, keepdims=False)
        grad_seq = lax.dynamic_index_in_dim(grad_all, sequence, 0, keepdims=False)
        stats_seq = lax.dynamic_index_in_dim(stats_all, sequence, 0, keepdims=False)

        def one_one_block(carried, number):
            key_grad, value_grad = carried
            row_start = number * block_rows
            query_block = lax.dynamic_slice_in_dim(query_seq, row_start, block_rows, 0)
            grad_block = lax.dynamic_slice_in_dim(grad_seq, row_start, block_rows, 0)
            stats_block = lax.dynamic_index_in_dim(stats_seq, number, 0, keepdims=False)
            scores = block_scores(query_block, key_rows, row_start, block_rows, labels)
            probability = jnp.exp(scores - stats_block[..., None])
            value_grad = value_grad + jnp.einsum(
                "hqk,qhd->khd",
                probability.astype(jnp.bfloat16),
                grad_block,
                preferred_element_type=jnp.float32,
            )
            grad_prob = jnp.einsum(
                "qhd,khd->hqk", grad_block, value_rows, preferred_element_type=jnp.float32
            )
            inner = jnp.sum(grad_prob * probability, -1, keepdims=True)
            grad_scores = (probability * (grad_prob - inner)).astype(jnp.bfloat16)
            query_grad = jnp.einsum(
                "hqk,khd->qhd", grad_scores, key_rows, preferred_element_type=jnp.float32
            ) * HD ** (-0.5)
            key_grad = key_grad + jnp.einsum(
                "hqk,qhd->khd", grad_scores, query_block, preferred_element_type=jnp.float32
            ) * HD ** (-0.5)
            return ((key_grad, value_grad), query_grad)

        zero_grad = jnp.zeros(key_rows.shape, jnp.float32)
        (key_grad, value_grad), query_grad = lax.scan(
            one_one_block, (zero_grad, zero_grad), jnp.arange(per_sequence, dtype=jnp.int32)
        )
        return (query_grad.reshape(key_rows.shape), key_grad, value_grad)

    query_grad, key_grad, value_grad = lax.map(one_sequence, jnp.arange(sequences, dtype=jnp.int32))
    return (
        query_grad.reshape(query_flat.shape),
        key_grad.reshape(query_flat.shape),
        value_grad.reshape(query_flat.shape),
    )


def local(
    tokens,
    segments,
    ln1_gain,
    ln1_bias,
    w_query,
    q_bias,
    w_key,
    w_value,
    v_bias,
    w_out,
    out_bias,
    ln2_gain,
    ln2_bias,
    w_up,
    up_bias,
    w_down,
    down_bias,
    cotangent,
):
    f32 = jnp.float32
    bf16 = jnp.bfloat16
    heads_width = w_query.shape[1]
    gain_one = ln1_gain.astype(f32)
    gain_two = ln2_gain.astype(f32)
    resid = jnp.transpose(tokens).astype(f32)
    cot_rows = jnp.transpose(cotangent)
    own_count = segments.shape[0] // lax.axis_size("col")
    own_segments = lax.dynamic_slice_in_dim(
        segments, lax.axis_index("col") * own_count, own_count, 0
    )
    normed_a, hat_a, inverse_a = norm_forward(resid, gain_one, ln1_bias.astype(f32))
    gathered_a = gather_rows(normed_a)
    w_joint = jnp.concatenate([w_query, w_key, w_value], 1)
    joint_bias = jnp.concatenate(
        [q_bias.astype(f32), jnp.zeros(heads_width, f32), v_bias.astype(f32)]
    )
    joint = (product_columns(gathered_a, w_joint) + joint_bias).astype(bf16)
    query_rows = joint[:, :heads_width]
    key_rows = joint[:, heads_width : 2 * heads_width]
    value_rows = joint[:, 2 * heads_width :]
    attended, log_totals = attend_forward(query_rows, key_rows, value_rows, own_segments)
    gathered_o = gather_columns(attended)
    hidden = resid + product_rows(gathered_o, w_out) + out_bias.astype(f32)
    normed_b, hat_b, inverse_b = norm_forward(hidden, gain_two, ln2_bias.astype(f32))
    gathered_b = gather_rows(normed_b)
    pre_act = product_columns(gathered_b, w_up) + up_bias.astype(f32)
    activated = jax.nn.gelu(pre_act).astype(bf16)
    gathered_u = gather_columns(activated)
    result = hidden + product_rows(gathered_u, jnp.transpose(w_down)) + down_bias.astype(f32)
    grad_out_all = gather_rows(cot_rows)
    grad_down = jnp.einsum("td,tf->df", grad_out_all, gathered_u, preferred_element_type=f32)
    grad_down_bias = jnp.sum(grad_out_all, 0, dtype=f32)
    grad_act = product_columns(grad_out_all, w_down)
    _, gelu_pull = jax.vjp(jax.nn.gelu, pre_act)
    grad_pre = gelu_pull(grad_act)[0].astype(bf16)
    grad_pre_all = gather_columns(grad_pre)
    grad_up = jnp.einsum("td,tf->df", gathered_b, grad_pre_all, preferred_element_type=f32)
    grad_up_bias = jnp.sum(grad_pre_all, 0, dtype=f32)
    grad_b = product_rows(grad_pre_all, jnp.transpose(w_up))
    two_gain_part = jnp.sum(grad_b * hat_b, 0)
    two_shift_part = jnp.sum(grad_b, 0)
    grad_hidden = cot_rows.astype(f32) + norm_backward(grad_b, hat_b, inverse_b, gain_two)
    grad_branch_all = gather_rows(grad_hidden.astype(bf16))
    grad_out = jnp.einsum("th,td->hd", gathered_o, grad_branch_all, preferred_element_type=f32)
    grad_out_bias = jnp.sum(grad_branch_all, 0, dtype=f32)
    grad_attended = product_columns(grad_branch_all, jnp.transpose(w_out)).astype(bf16)
    query_grad, key_grad, value_grad = attend_backward(
        query_rows, key_rows, value_rows, grad_attended, log_totals, own_segments
    )
    grad_joint = jnp.concatenate(
        [query_grad.astype(bf16), key_grad.astype(bf16), value_grad.astype(bf16)], 1
    )
    grad_joint_all = gather_columns(grad_joint)
    grad_joint_weight = jnp.einsum(
        "td,tf->df", gathered_a, grad_joint_all, preferred_element_type=f32
    )
    grad_query_bias = jnp.sum(grad_joint_all[:, :heads_width], 0, dtype=f32)
    grad_value_bias = jnp.sum(grad_joint_all[:, 2 * heads_width :], 0, dtype=f32)
    grad_a = product_rows(grad_joint_all, jnp.transpose(w_joint))
    one_gain_part = jnp.sum(grad_a * hat_a, 0)
    one_shift_part = jnp.sum(grad_a, 0)
    grad_input = grad_hidden + norm_backward(grad_a, hat_a, inverse_a, gain_one)
    (
        joint_sum,
        query_bias_sum,
        value_bias_sum,
        out_sum,
        out_bias_sum,
        up_sum,
        up_bias_sum,
        down_sum,
        down_bias_sum,
    ) = (
        lax.psum(grad_joint_weight.astype(jnp.bfloat16), "dp").astype(jnp.float32),
        lax.psum(grad_query_bias.astype(jnp.bfloat16), "dp").astype(jnp.float32),
        lax.psum(grad_value_bias.astype(jnp.bfloat16), "dp").astype(jnp.float32),
        lax.psum(grad_out.astype(jnp.bfloat16), "dp").astype(jnp.float32),
        lax.psum(grad_out_bias.astype(jnp.bfloat16), "dp").astype(jnp.float32),
        lax.psum(grad_up.astype(jnp.bfloat16), "dp").astype(jnp.float32),
        lax.psum(grad_up_bias.astype(jnp.bfloat16), "dp").astype(jnp.float32),
        lax.psum(grad_down.astype(jnp.bfloat16), "dp").astype(jnp.float32),
        lax.psum(grad_down_bias.astype(jnp.bfloat16), "dp").astype(jnp.float32),
    )
    one_gain_sum, one_shift_sum, two_gain_sum, two_shift_sum = lax.psum(
        (one_gain_part, one_shift_part, two_gain_part, two_shift_part), ("dp", "row")
    )
    return (
        jnp.transpose(result.astype(bf16)),
        jnp.transpose(grad_input),
        one_gain_sum,
        one_shift_sum,
        joint_sum[:, :heads_width],
        query_bias_sum,
        joint_sum[:, heads_width : 2 * heads_width],
        joint_sum[:, 2 * heads_width :],
        value_bias_sum,
        out_sum,
        out_bias_sum,
        two_gain_sum,
        two_shift_sum,
        up_sum,
        up_bias_sum,
        down_sum,
        down_bias_sum,
    )


def solution(mesh):
    placed = (
        P("col", ("dp", "row")),
        P("dp", None),
        P("col"),
        P("col"),
        P("col", "row"),
        P("row"),
        P("col", "row"),
        P("col", "row"),
        P("row"),
        P("row", "col"),
        P("col"),
        P("col"),
        P("col"),
        P("col", "row"),
        P("row"),
        P("col", "row"),
        P("col"),
        P("col", ("dp", "row")),
    )
    return jax.shard_map(
        local,
        mesh=mesh,
        in_specs=placed,
        out_specs=(
            P("col", ("dp", "row")),
            P("col", ("dp", "row")),
            P("col"),
            P("col"),
            P("col", "row"),
            P("row"),
            P("col", "row"),
            P("col", "row"),
            P("row"),
            P("row", "col"),
            P("col"),
            P("col"),
            P("col"),
            P("col", "row"),
            P("row"),
            P("col", "row"),
            P("col"),
        ),
        check_vma=False,
    )
```

profile of v0, /device:TPU:0, one launch (start us, length us, event | category | flops | bytes accessed | tf_op | source)
XLA Modules:
  0.0 2544.1 jit_solution(8207229807388879520)
XLA Ops:
  11.3 20.5 all-reduce.4
  34.8 26.9 %all-gather.9.cloned.1.call-done = bf16[8192,192]{0,1:T(8,128)(2,1)} async-done(((bf16[2048,192]{0,1:T(8,128)(2,1)}), bf16[8192,192]{0,1:T(8,128)(2,1)}) %all-gather.9.cloned.1.call-update) | async-done | bytes 3145744 | tf_op jit(solution)/shard_map/all_gather | solution.py:18
  61.7 11.1 fusion.70
  74.3 312.5 %reduce-scatter.9.cloned.1.call-done = f32[2048,576]{0,1:T(8,128)} async-done(((f32[8192,576]{0,1:T(8,128)}), f32[2048,576]{0,1:T(8,128)}) %reduce-scatter.9.cloned.1.call-update) | async-done | bytes 4718608 | tf_op jit(solution)/shard_map/reduce_scatter | solution.py:31
  389.7 97.0 %while.40 = (s32[]{:T(128)}, bf16[4,512,3,64]{1,3,2,0:T(8,128)(2,1)}, f32[4,3,512]{2,1,0:T(4,128)}, s32[4]{0:T(128)S(1)}, s32[1,2048]{1,0:T(1,128)S(1)}, /*index...) while((s32[]{:T(128)}, ...), condition=%wide.region_8.9_spmd, body=%wide.region_5.8_spmd.sunk | while | flops 846298112 | bytes 43979080 | solution.py:115
  489.9 64.6 %all-gather.11.cloned.1.call-done = bf16[8192,192]{0,1:T(8,128)(2,1)} async-done(((bf16[2048,192]{0,1:T(8,128)(2,1)}), bf16[8192,192]{0,1:T(8,128)(2,1)}) %all-gather.11.cloned.1.call-update) | async-done | bytes 3145744 | tf_op jit(solution)/shard_map/all_gather | solution.py:22
  562.8 54.6 %reduce-scatter.11.cloned.1.call-done = f32[2048,192]{0,1:T(8,128)} async-done(((f32[8192,192]{0,1:T(8,128)}), f32[2048,192]{0,1:T(8,128)}) %reduce-scatter.11.cloned.1.call-update) | async-done | bytes 1572880 | tf_op jit(solution)/shard_map/reduce_scatter | solution.py:45
  620.0 19.3 all-reduce.3
  647.4 14.8 fusion.81
  662.2 15.7 all-gather.13.cloned.1.call-done
  677.9 14.9 fusion.79
  694.2 400.5 %reduce-scatter.17.cloned.1.call-done = f32[2048,768]{1,0:T(8,128)} async-done(((f32[8192,768]{1,0:T(8,128)}), f32[2048,768]{1,0:T(8,128)}) %reduce-scatter.17.cloned.1.call-update) | async-done | bytes 6291472 | tf_op jit(solution)/shard_map/reduce_scatter | solution.py:31
  1094.7 418.7 %reduce-scatter.13.cloned.1.call-done = f32[2048,768]{1,0:T(8,128)} async-done(((f32[8192,768]{1,0:T(8,128)}), f32[2048,768]{1,0:T(8,128)}) %reduce-scatter.13.cloned.1.call-update) | async-done | bytes 6291472 | tf_op jit(solution)/shard_map/reduce_scatter | solution.py:31
  1513.4 9.4 fusion.48
  1522.9 220.1 %all-gather.19.cloned.1.call-done = bf16[8192,768]{1,0:T(8,128)(2,1)} async-done(((bf16[2048,768]{1,0:T(8,128)(2,1)}), bf16[8192,768]{1,0:T(8,128)(2,1)}) %all-gather.19.cloned.1.call-update) | async-done | bytes 12582928 | tf_op jit(solution)/shard_map/all_gather | solution.py:22
  1743.0 11.4 fusion.82
  1754.5 56.7 %reduce-scatter.19.cloned.1.call-done = f32[2048,192]{0,1:T(8,128)} async-done(((f32[8192,192]{0,1:T(8,128)}), f32[2048,192]{0,1:T(8,128)}) %reduce-scatter.19.cloned.1.call-update) | async-done | bytes 1572880 | tf_op jit(solution)/shard_map/reduce_scatter | solution.py:45
  1813.8 18.7 all-reduce.2
  1835.6 25.9 %all-gather.21.cloned.1.call-done = bf16[8192,192]{0,1:T(8,128)(2,1)} async-done(((bf16[2048,192]{0,1:T(8,128)(2,1)}), bf16[8192,192]{0,1:T(8,128)(2,1)}) %all-gather.21.cloned.1.call-update) | async-done | bytes 3145744 | tf_op jit(solution)/shard_map/all_gather | solution.py:18
  1867.9 110.1 %reduce-scatter.21.cloned.1.call-done = f32[2048,192]{0,1:T(8,128)} async-done(((f32[8192,192]{0,1:T(8,128)}), f32[2048,192]{0,1:T(8,128)}) %reduce-scatter.21.cloned.1.call-update) | async-done | bytes 1572880 | tf_op jit(solution)/shard_map/reduce_scatter | solution.py:31
  1979.6 153.1 %while.41 = (s32[]{:T(128)}, f32[2048,3,64]{0,2,1:T(8,128)}, f32[2048,3,64]{0,2,1:T(8,128)}, bf16[4,512,3,64]{1,3,2,0:T(8,128)(2,1)}, s32[4]{0:T(128)S(1)}, /*in...) while((s32[]{:T(128)}, f32[2048,3,64]{0,2,1:T(8,128)}, ...), condition=%wide.region_25.26_spmd.clone, body=%wide.region_23.25_spmd.clone.sunk | while | flops 2065660928 | bytes 156695056 | solution.py:167
  2138.1 9.0 convolution_convert_fusion.1
  2147.1 51.3 %all-gather.15.cloned.1.call-done = bf16[8192,768]{1,0:T(8,128)(2,1)} async-done(((bf16[2048,768]{1,0:T(8,128)(2,1)}), bf16[8192,768]{1,0:T(8,128)(2,1)}) %all-gather.15.cloned.1.call-update) | async-done | bytes 12582928 | tf_op jit(solution)/shard_map/all_gather | solution.py:22
  2198.5 8.0 fusion.67
  2208.1 156.8 %all-gather.23.cloned.1.call-done = bf16[8192,576]{0,1:T(8,128)(2,1)} async-done(((bf16[2048,576]{0,1:T(8,128)(2,1)}), bf16[8192,576]{0,1:T(8,128)(2,1)}) %all-gather.23.cloned.1.call-update) | async-done | bytes 9437200 | tf_op jit(solution)/shard_map/all_gather | solution.py:22
  2365.0 8.9 convolution_convert_fusion.2
  2374.0 9.1 fusion.69
  2384.0 11.4 fusion.80
  2423.3 47.8 %reduce-scatter.23.cloned.1.call-done = f32[2048,192]{0,1:T(8,128)} async-done(((f32[8192,192]{0,1:T(8,128)}), f32[2048,192]{0,1:T(8,128)}) %reduce-scatter.23.cloned.1.call-update) | async-done | bytes 1572880 | tf_op jit(solution)/shard_map/reduce_scatter | solution.py:45
  2473.3 13.3 all-reduce
  2486.6 18.7 all-reduce.1
  2505.3 26.8 %reduce-scatter.15.cloned.1.call-done = f32[2048,192]{0,1:T(8,128)} async-done(((f32[8192,192]{0,1:T(8,128)}), f32[2048,192]{0,1:T(8,128)}) %reduce-scatter.15.cloned.1.call-update) | async-done | bytes 1572880 | tf_op jit(solution)/shard_map/reduce_scatter | solution.py:45
  (326 shorter events, 312.5 us)
Async XLA Ops:
  7.2 670.7 %copy-start = (bf16[192,768]{1,0:T(8,128)(2,1)S(1)}, bf16[192,768]{1,0:T(8,128)(2,1)}, u32[]{:S(2)}) copy-start(bf16[192,768]{1,0:T(8,128)(2,1)} %param.35) | copy-start | bytes 884740
  7.2 54.4 %all-gather.9.cloned.1.call-start = ((), (), s32[]{:S(2)}) async-start(), calls=%async_computation.8 | async-start | bytes 3932160 | tf_op jit(solution)/shard_map/all_gather | solution.py:18
  34.7 352.0 %reduce-scatter.9.cloned.1.call-start = ((), (), s32[]{:S(2)}) async-start(), calls=%async_computation.9 | async-start | bytes 23592960 | tf_op jit(solution)/shard_map/reduce_scatter | solution.py:31
  72.8 481.8 %all-gather.11.cloned.1.call-start = ((), (), s32[]{:S(2)}) async-start(), calls=%async_computation.10 | async-start | bytes 3932160 | tf_op jit(solution)/shard_map/all_gather | solution.py:22
  486.7 73.4 %copy-start.15 = (bf16[1,2048,3,64]{1,3,2,0:T(8,128)(2,1)}, bf16[1,2048,3,64]{1,3,2,0:T(8,128)(2,1)S(1)}, u32[]{:S(2)}) copy-start(bf16[1,2048,3,64]{1,3,2,0:T(8,128)(2,1)S(1)} %get-tuple-element.608) | copy-start | bytes 2359300
  486.7 67.8 %copy-start.21 = (bf16[192,192]{1,0:T(8,128)(2,1)S(1)}, bf16[192,192]{1,0:T(8,128)(2,1)}, u32[]{:S(2)}) copy-start(bf16[192,192]{1,0:T(8,128)(2,1)} %param.31) | copy-start | bytes 221188
  489.9 127.5 %reduce-scatter.11.cloned.1.call-start = ((), (), s32[]{:S(2)}) async-start(), calls=%async_computation.11 | async-start | bytes 7864320 | tf_op jit(solution)/shard_map/reduce_scatter | solution.py:45
  560.2 87.2 %all-gather.17.cloned.1.call-start = ((), (), s32[]{:S(2)}) async-start(), calls=%async_computation.16 | async-start | bytes 3932160 | tf_op jit(solution)/shard_map/all_gather | solution.py:18
  560.8 117.1 %all-gather.13.cloned.1.call-start = ((), (), s32[]{:S(2)}) async-start(), calls=%async_computation.12 | async-start | bytes 3932160 | tf_op jit(solution)/shard_map/all_gather | solution.py:18
  620.0 1212.6 %copy-start.9 = (f32[2048,192]{0,1:T(8,128)}, f32[2048,192]{0,1:T(8,128)S(1)}, u32[]{:S(2)}) copy-start(f32[2048,192]{0,1:T(8,128)S(1)} %get-tuple-element.321) | copy-start | bytes 4718596
  640.0 1192.6 %copy-start.28 = (f32[2048]{0:T(1024)}, f32[2048]{0:T(1024)S(1)}, u32[]{:S(2)}) copy-start(f32[2048]{0:T(1024)S(1)} %get-tuple-element.336) | copy-start | bytes 24580
  642.5 452.2 %reduce-scatter.17.cloned.1.call-start = ((), (), s32[]{:S(2)}) async-start(), calls=%async_computation.17 | async-start | bytes 31457280 | tf_op jit(solution)/shard_map/reduce_scatter | solution.py:31
  662.2 851.2 %reduce-scatter.13.cloned.1.call-start = ((), (), s32[]{:S(2)}) async-start(), calls=%async_computation.13 | async-start | bytes 31457280 | tf_op jit(solution)/shard_map/reduce_scatter | solution.py:31
  692.8 1050.2 %all-gather.19.cloned.1.call-start = ((), (), s32[]{:S(2)}) async-start(), calls=%async_computation.18 | async-start | bytes 15728640 | tf_op jit(solution)/shard_map/all_gather | solution.py:22
  1522.9 288.3 %reduce-scatter.19.cloned.1.call-start = ((), (), s32[]{:S(2)}) async-start(), calls=%async_computation.19 | async-start | bytes 7864320 | tf_op jit(solution)/shard_map/reduce_scatter | solution.py:45
  1754.4 107.1 %all-gather.21.cloned.1.call-start = ((), (), s32[]{:S(2)}) async-start(), calls=%async_computation.20 | async-start | bytes 3932160 | tf_op jit(solution)/shard_map/all_gather | solution.py:18
  1835.6 142.4 %reduce-scatter.21.cloned.1.call-start = ((), (), s32[]{:S(2)}) async-start(), calls=%async_computation.21 | async-start | bytes 7864320 | tf_op jit(solution)/shard_map/reduce_scatter | solution.py:31
  1867.1 331.3 %all-gather.15.cloned.1.call-start = ((), (), s32[]{:S(2)}) async-start(), calls=%async_computation.14 | async-start | bytes 15728640 | tf_op jit(solution)/shard_map/all_gather | solution.py:22
  1867.9 497.1 %all-gather.23.cloned.1.call-start = ((), (), s32[]{:S(2)}) async-start(), calls=%async_computation.22 | async-start | bytes 11796480 | tf_op jit(solution)/shard_map/all_gather | solution.py:22
  2138.1 277.9 %all-reduce.9.cloned.1.call-start = ((), (), s32[]{:S(2)}) async-start(), calls=%async_computation.24 | async-start | bytes 1867776 | tf_op jit(solution)/shard_map/psum | solution.py:274
  2208.1 165.8 %copy-start.23 = (bf16[192,192]{1,0:T(8,128)(2,1)S(1)}, bf16[192,192]{1,0:T(8,128)(2,1)}, u32[]{:S(2)}) copy-start(bf16[192,192]{1,0:T(8,128)(2,1)} %param.29) | copy-start | bytes 221188
  2208.1 165.8 %copy-start.25 = (bf16[192,192]{1,0:T(8,128)(2,1)S(1)}, bf16[192,192]{1,0:T(8,128)(2,1)}, u32[]{:S(2)}) copy-start(bf16[192,192]{1,0:T(8,128)(2,1)} %param.28) | copy-start | bytes 221188
  2208.1 165.8 %copy-start.27 = (bf16[192,192]{1,0:T(8,128)(2,1)S(1)}, bf16[192,192]{1,0:T(8,128)(2,1)}, u32[]{:S(2)}) copy-start(bf16[192,192]{1,0:T(8,128)(2,1)} %param.26) | copy-start | bytes 221188
  2373.9 97.3 %reduce-scatter.23.cloned.1.call-start = ((), (), s32[]{:S(2)}) async-start(), calls=%async_computation.23 | async-start | bytes 7864320 | tf_op jit(solution)/shard_map/reduce_scatter | solution.py:45
  2383.0 149.1 %reduce-scatter.15.cloned.1.call-start = ((), (), s32[]{:S(2)}) async-start(), calls=%async_computation.15 | async-start | bytes 7864320 | tf_op jit(solution)/shard_map/reduce_scatter | solution.py:45
  2407.8 124.3 %copy-start.10 = (f32[2048,192]{0,1:T(8,128)S(1)}, f32[2048,192]{0,1:T(8,128)}, u32[]{:S(2)}) copy-start(f32[2048,192]{0,1:T(8,128)} %copy-done.9) | copy-start | bytes 4718596
  2407.8 124.3 %copy-start.16 = (bf16[192,2048]{1,0:T(8,128)(2,1)S(1)}, bf16[192,2048]{1,0:T(8,128)(2,1)}, u32[]{:S(2)}) copy-start(bf16[192,2048]{1,0:T(8,128)(2,1)} %param.39) | copy-start | bytes 2359300
  2407.8 124.3 %copy-start.29 = (f32[2048]{0:T(1024)S(1)}, f32[2048]{0:T(1024)}, u32[]{:S(2)}) copy-start(f32[2048]{0:T(1024)} %copy-done.28) | copy-start | bytes 24580
  2407.8 124.3 %copy-start.32 = (f32[2048]{0:T(1024)S(1)}, f32[2048]{0:T(1024)}, u32[]{:S(2)}) copy-start(f32[2048]{0:T(1024)} %copy-done.30) | copy-start | bytes 24580
  2407.8 124.3 %copy-start.38 = (f32[2048]{0:T(1024)S(1)}, f32[2048]{0:T(1024)}, u32[]{:S(2)}) copy-start(f32[2048]{0:T(1024)} %copy-done.37) | copy-start | bytes 24580
  2407.8 124.3 %copy-start.40 = (f32[2048]{0:T(1024)S(1)}, f32[2048]{0:T(1024)}, u32[]{:S(2)}) copy-start(f32[2048]{0:T(1024)} %copy-done.39) | copy-start | bytes 24580
  2407.9 124.3 %copy-start.42 = (f32[192]{0:T(256)S(1)}, f32[192]{0:T(256)}, u32[]{:S(2)}) copy-start(f32[192]{0:T(256)} %convert_element_type.160) | copy-start | bytes 2308
  (62 other events, 1100.8 us)
Sparse Core Ops, SparseCore 0:
  34.9 26.7 all-gather.8
  72.9 313.7 reduce-scatter.8
  490.0 64.5 all-gather.10
  560.3 57.0 reduce-scatter.10
  618.8 28.5 all-gather.16
  649.3 28.5 all-gather.12
  680.3 414.3 reduce-scatter.16
  1097.2 416.1 reduce-scatter.12
  1523.0 220.0 all-gather.18
  1754.6 56.5 reduce-scatter.18
  1835.7 25.7 all-gather.20
  1867.3 110.7 reduce-scatter.20
  1979.7 218.7 all-gather.14
  2200.0 164.9 all-gather.22
  2374.0 36.2 all-reduce.8
  2412.7 58.4 reduce-scatter.22
  2473.7 58.3 reduce-scatter.14
where the time goes:
time: 2550 us; the launch traced here: 2540 us
  waiting for transfers between devices  2000 us (78%)
  matrix products  262 us (10%)
  other arithmetic  126 us (5%)
  blocking collectives  95.6 us (4%)
  loops' own time  29.2 us (1%)
    reduce_scatter x4, waiting for transfers between devices, product_columns(): lax.psum_scatter(partial_term(jnp.int32(0), own_rows * lax.axis_size('col...  1240 us
    all_gather x4, waiting for transfers between devices, gather_columns(): return lax.all_gather(activation, 'col', axis=0, tiled=True)  493 us
    reduce_scatter x4, waiting for transfers between devices, product_rows(): lax.psum_scatter(partial_term(jnp.int32(0), own_rows * lax.axis_size('row...  186 us
    dot_general x8, matrix products, partial_term(): return jnp.dot(gathered, weight, preferred_element_type=jnp.float32)  83.8 us
    psum x4, blocking collectives, col_totals(): return lax.psum((first_sum, second_sum), 'col')  77.2 us
    all_gather x4, waiting for transfers between devices, gather_rows(): return lax.all_gather(activation, 'row', axis=0, tiled=True)  73.2 us
  transfers between devices with their start and end apart: 17, of which 16 were waited for; matrix products, arithmetic and copies ran while one was open for 9% of the time, Pallas kernels for 0%

commit v1 on v0

v1 whole, which is shorter than its diff:
```python
import functools

import jax
import jax.numpy as jnp
from jax import lax
from jax.experimental import pallas as pl
from jax.experimental.pallas import tpu as pltpu
from jax.sharding import PartitionSpec as P

HD = 64
EPS = 1e-05
NEG = -1000000000.0
BLOCK = 256
SCALE = HD ** (-0.5)
F32 = jnp.float32
BF16 = jnp.bfloat16


def contract(left, right, left_dim, right_dim):
    return lax.dot_general(
        left, right, (((left_dim,), (right_dim,)), ((), ())), preferred_element_type=F32
    )


def block_mask(query_block, key_block, query_labels, key_labels):
    shape = (BLOCK, BLOCK)
    key_places = key_block * BLOCK + lax.broadcasted_iota(jnp.int32, shape, 0)
    query_places = query_block * BLOCK + lax.broadcasted_iota(jnp.int32, shape, 1)
    return (query_places >= key_places) & (key_labels == query_labels)


def forward_kernel(heads, first_ref, seg_row, seg_col, q_ref, k_ref, v_ref, o_ref, lse_ref):
    i = pl.program_id(0)
    query_labels = seg_row[...]
    queries = [q_ref[h * HD : (h + 1) * HD, :] for h in range(heads)]

    def step(j, carried):
        start = pl.multiple_of(j * BLOCK, BLOCK)
        allowed = block_mask(i, j, query_labels, seg_col[pl.ds(start, BLOCK), :])
        after = []
        for h in range(heads):
            highest, total, acc = carried[h]
            scores = contract(k_ref[h, pl.ds(start, BLOCK), :], queries[h], 1, 0) * SCALE
            scores = jnp.where(allowed, scores, NEG)
            higher = jnp.maximum(highest, jnp.max(scores, 0, keepdims=True))
            shrink = jnp.exp(highest - higher)
            weights = jnp.exp(scores - higher)
            total = total * shrink + jnp.sum(weights, 0, keepdims=True)
            values = v_ref[h * HD : (h + 1) * HD, pl.ds(start, BLOCK)]
            acc = acc * shrink + contract(values, weights.astype(BF16), 1, 0)
            after.append((higher, total, acc))
        return tuple(after)

    empty = (
        jnp.full((1, BLOCK), NEG, F32),
        jnp.zeros((1, BLOCK), F32),
        jnp.zeros((HD, BLOCK), F32),
    )
    carried = lax.fori_loop(first_ref[i], i + 1, step, (empty,) * heads)
    lse_ref[...] = jnp.zeros_like(lse_ref)
    for h in range(heads):
        highest, total, acc = carried[h]
        o_ref[h * HD : (h + 1) * HD, :] = (acc / total).astype(BF16)
        lse_ref[h : h + 1, :] = highest + jnp.log(total)


def attend_forward(queries, key_rows, values, labels):
    width, length = queries.shape
    heads = width // HD
    starts = labels[::BLOCK]
    first = jnp.sum(labels[None, :] < starts[:, None], 1, dtype=jnp.int32) // BLOCK
    return pl.pallas_call(
        functools.partial(forward_kernel, heads),
        grid_spec=pltpu.PrefetchScalarGridSpec(
            num_scalar_prefetch=1,
            grid=(length // BLOCK,),
            in_specs=[
                pl.BlockSpec((1, BLOCK), lambda i, first: (0, i)),
                pl.BlockSpec((length, 1), lambda i, first: (0, 0)),
                pl.BlockSpec((width, BLOCK), lambda i, first: (0, i)),
                pl.BlockSpec((heads, length, HD), lambda i, first: (0, 0, 0)),
                pl.BlockSpec((width, length), lambda i, first: (0, 0)),
            ],
            out_specs=[
                pl.BlockSpec((width, BLOCK), lambda i, first: (0, i)),
                pl.BlockSpec((8, BLOCK), lambda i, first: (0, i)),
            ],
        ),
        out_shape=[
            jax.ShapeDtypeStruct((width, length), BF16),
            jax.ShapeDtypeStruct((8, length), F32),
        ],
        compiler_params=pltpu.CompilerParams(vmem_limit_bytes=40 * 2**20),
        cost_estimate=pl.CostEstimate(
            flops=2 * width * length * length, bytes_accessed=4 * 2 * width * length,
            transcendentals=heads * length * length // 2,
        ),
        name="attend_forward",
    )(first, labels[None, :], labels[:, None], queries, key_rows, values)


def backward_kernel(
    heads, last_ref, seg_row, seg_col, k_ref, v_ref, kt_ref, q_ref, g_ref, lse_ref, delta_ref,
    dq_ref, dk_ref, dv_ref, dq_sum,
):
    j = pl.program_id(0)
    key_labels = seg_col[...]

    @pl.when(j == 0)
    def _():
        dq_sum[...] = jnp.zeros_like(dq_sum)

    def step(i, carried):
        start = pl.multiple_of(i * BLOCK, BLOCK)
        span = pl.ds(start, BLOCK)
        allowed = block_mask(i, j, seg_row[:, span], key_labels)
        after = []
        for h in range(heads):
            dk, dv = carried[h]
            part = slice(h * HD, (h + 1) * HD)
            queries = q_ref[part, span]
            grads = g_ref[part, span]
            scores = contract(k_ref[h], queries, 1, 0) * SCALE
            probs = jnp.exp(jnp.where(allowed, scores - lse_ref[h : h + 1, span], NEG))
            grad_probs = contract(v_ref[h], grads, 1, 0)
            grad_scores = (probs * (grad_probs - delta_ref[h : h + 1, span])).astype(BF16)
            dv = dv + contract(grads, probs.astype(BF16), 1, 1)
            dk = dk + contract(queries, grad_scores, 1, 1)
            dq_sum[part, span] += contract(kt_ref[part, :], grad_scores, 1, 0)
            after.append((dk, dv))
        return tuple(after)

    zero = jnp.zeros((HD, BLOCK), F32)
    carried = lax.fori_loop(j, last_ref[j], step, ((zero, zero),) * heads)
    for h in range(heads):
        part = slice(h * HD, (h + 1) * HD)
        dk_ref[part, :] = (carried[h][0] * SCALE).astype(BF16)
        dv_ref[part, :] = carried[h][1].astype(BF16)

    @pl.when(j == pl.num_programs(0) - 1)
    def _():
        dq_ref[...] = (dq_sum[...] * SCALE).astype(BF16)


def attend_backward(queries, keys, key_rows, value_rows, grads, lse, delta, labels):
    width, length = queries.shape
    heads = width // HD
    ends = labels[BLOCK - 1 :: BLOCK]
    last = (
        jnp.sum(labels[None, :] <= ends[:, None], 1, dtype=jnp.int32) + BLOCK - 1
    ) // BLOCK
    rows = pl.BlockSpec((heads, BLOCK, HD), lambda j, last: (0, j, 0))
    whole = pl.BlockSpec((width, length), lambda j, last: (0, 0))
    piece = pl.BlockSpec((width, BLOCK), lambda j, last: (0, j))
    stats = pl.BlockSpec((8, length), lambda j, last: (0, 0))
    return pl.pallas_call(
        functools.partial(backward_kernel, heads),
        grid_spec=pltpu.PrefetchScalarGridSpec(
            num_scalar_prefetch=1,
            grid=(length // BLOCK,),
            in_specs=[
                pl.BlockSpec((1, length), lambda j, last: (0, 0)),
                pl.BlockSpec((BLOCK, 1), lambda j, last: (j, 0)),
                rows,
                rows,
                piece,
                whole,
                whole,
                stats,
                stats,
            ],
            out_specs=[whole, piece, piece],
            scratch_shapes=[pltpu.VMEM((width, length), F32)],
        ),
        out_shape=[jax.ShapeDtypeStruct((width, length), BF16)] * 3,
        compiler_params=pltpu.CompilerParams(vmem_limit_bytes=40 * 2**20),
        cost_estimate=pl.CostEstimate(
            flops=5 * width * length * length, bytes_accessed=8 * 2 * width * length,
            transcendentals=heads * length * length // 2,
        ),
        name="attend_backward",
    )(last, labels[None, :], labels[:, None], key_rows, value_rows, keys, queries, grads, lse, delta)


def head_rows(columns):
    return jnp.transpose(columns.reshape(-1, HD, columns.shape[1]), (0, 2, 1))


def swap(array, bit):
    count = lax.axis_size("row")
    return lax.ppermute(array, "row", [(place, place ^ bit) for place in range(count)])


def add_other_dp(array):
    return array.astype(F32) + lax.ppermute(array, "dp", [(0, 1), (1, 0)]).astype(F32)


def norm_stats(values):
    center = jnp.mean(values, 0, keepdims=True)
    offset = values - center
    return center, lax.rsqrt(jnp.mean(offset * offset, 0, keepdims=True) + EPS)


def own_block(full, place, width, axis):
    return lax.dynamic_slice_in_dim(full, place * width, width, axis)


def put_block(block, place, count):
    blank = jnp.zeros((block.shape[0] * count,), F32)
    return lax.dynamic_update_slice(blank, block, (place * block.shape[0],))


def local(
    tokens, segments, ln1_gain, ln1_bias, w_query, q_bias, w_key, w_value, v_bias, w_out,
    out_bias, ln2_gain, ln2_bias, w_up, up_bias, w_down, down_bias, cotangent,
):
    cols, rows = lax.axis_size("col"), lax.axis_size("row")
    length = segments.shape[1]
    held = tokens.shape[1]
    seqs = held // length
    group = cols // seqs
    own = held // cols
    features = tokens.shape[0]
    wide = features * cols
    block = w_query.shape[1]
    hidden_block = w_up.shape[1]
    r, c = lax.axis_index("row"), lax.axis_index("col")
    seq, place = c // group, c % group
    head = r ^ place
    groups = None
    if seqs > 1:
        groups = [[s * group + g for g in range(group)] for s in range(seqs)]
    mixed = [
        (a * cols + b, (a ^ (b % group)) * cols + b) for a in range(rows) for b in range(cols)
    ]

    vectors = jnp.stack([ln1_gain, ln1_bias, ln2_gain, ln2_bias, out_bias, down_bias], 1)
    first_pack = jnp.concatenate([w_query, w_key, w_value, vectors], 1)
    first_all = lax.all_gather(first_pack, "col", axis=0, tiled=True)
    x_all = lax.all_gather(tokens, "col", axis=0, tiled=True)
    w_joint = lax.ppermute(first_all[:, : 3 * block], ("row", "col"), mixed)
    vecs = first_all[:, 3 * block :].astype(F32)
    gain_one, shift_one, gain_two, shift_two, bias_out, bias_down = (
        vecs[:, n : n + 1] for n in range(6)
    )
    row_biases = lax.all_gather(jnp.concatenate([q_bias, v_bias, up_bias]), "row", axis=0)
    row_biases = row_biases.astype(F32)
    head_bias = lax.dynamic_index_in_dim(row_biases, head, 0, keepdims=False)
    joint_bias = jnp.concatenate(
        [head_bias[:block], jnp.zeros((block,), F32), head_bias[block : 2 * block]]
    )
    bias_up = jnp.concatenate(
        [
            lax.dynamic_index_in_dim(row_biases, who, 0, keepdims=False)[2 * block :]
            for who in (r, r ^ 2)
        ]
    )
    second_pack = jnp.concatenate([w_up, w_down, jnp.transpose(w_out)], 1)
    second_all = lax.all_gather(second_pack, "col", axis=0, tiled=True)
    up_down = second_all[:, : 2 * hidden_block]
    up_down_other = swap(up_down, 2)
    weight_up = jnp.concatenate(
        [up_down[:, :hidden_block], up_down_other[:, :hidden_block]], 1
    )
    weight_down = jnp.concatenate(
        [up_down[:, hidden_block:], up_down_other[:, hidden_block:]], 1
    )
    out_blocks = lax.all_gather(second_all[:, 2 * hidden_block :], "row", axis=0)
    weight_out = jnp.concatenate(
        [lax.dynamic_index_in_dim(out_blocks, r ^ g, 0, keepdims=False) for g in range(group)], 1
    )

    labels = lax.dynamic_index_in_dim(segments, r * seqs + seq, 0, keepdims=False)
    center_all, inverse_all = norm_stats(x_all.astype(F32))
    center = own_block(center_all, seq, length, 1)
    inverse = own_block(inverse_all, seq, length, 1)
    hat_a = (own_block(x_all, seq, length, 1).astype(F32) - center) * inverse
    normed_a = (hat_a * gain_one + shift_one).astype(BF16)
    joint = (contract(w_joint, normed_a, 0, 0) + joint_bias[:, None]).astype(BF16)
    queries, keys, values = joint[:block], joint[block : 2 * block], joint[2 * block :]
    key_rows, value_rows = head_rows(keys), head_rows(values)
    attended, lse = attend_forward(queries, key_rows, values, labels)

    att = lax.all_to_all(attended, "col", 1, 0, axis_index_groups=groups, tiled=True)
    ct_own = lax.all_to_all(cotangent, "col", 1, 0, tiled=True)
    ct_pair = jnp.concatenate([ct_own, swap(ct_own, 1)], 1)
    x_own = own_block(x_all, c, own, 1).astype(F32)
    hidden = x_own + contract(weight_out, att, 1, 0) + bias_out
    center_b, inverse_b = norm_stats(hidden)
    hat_b = (hidden - center_b) * inverse_b
    normed_b = (hat_b * gain_two + shift_two).astype(BF16)
    norm_pair = jnp.concatenate([normed_b, swap(normed_b, 1)], 1)
    pre_act = contract(weight_up, norm_pair, 0, 0) + bias_up[:, None]
    activated = jax.nn.gelu(pre_act).astype(BF16)
    down = contract(weight_down, activated, 1, 0)
    down = down[:, :own] + swap(down[:, own:].astype(BF16), 1).astype(F32)
    result = (hidden + down + bias_down).astype(BF16)
    out = lax.all_to_all(result, "col", 0, 1, tiled=True)

    grad_act = contract(weight_down, ct_pair, 0, 0)
    _, pull = jax.vjp(jax.nn.gelu, pre_act)
    grad_pre = pull(grad_act)[0].astype(BF16)
    grad_b = contract(weight_up, grad_pre, 1, 0)
    grad_b = grad_b[:, :own] + swap(grad_b[:, own:].astype(BF16), 1).astype(F32)
    scaled = grad_b * gain_two
    grad_hidden = ct_own.astype(F32) + inverse_b * (
        scaled
        - jnp.mean(scaled, 0, keepdims=True)
        - hat_b * jnp.mean(scaled * hat_b, 0, keepdims=True)
    )
    branch = grad_hidden.astype(BF16)
    grad_att = contract(weight_out, branch, 0, 0).astype(BF16)
    grad_att = lax.all_to_all(grad_att, "col", 0, 1, axis_index_groups=groups, tiled=True)
    hidden_cols = lax.all_to_all(branch, "col", 0, 1, tiled=True)

    down_grad = contract(ct_pair, activated, 1, 1)
    up_grad = contract(norm_pair, grad_pre, 1, 1)
    other = jnp.concatenate(
        [up_grad[:, hidden_block:].astype(BF16), down_grad[:, hidden_block:].astype(BF16)], 1
    )
    mine = jnp.concatenate([up_grad[:, :hidden_block], down_grad[:, :hidden_block]], 1)
    up_down_grad = (mine + swap(other, 2).astype(F32)).astype(BF16)
    out_grad = contract(branch, att, 1, 1).astype(BF16)
    out_grad = jnp.stack(
        [own_block(out_grad, r ^ h, block, 1) for h in range(rows)], 0
    )
    out_grad = lax.psum_scatter(out_grad, "row", scatter_dimension=0, tiled=False)
    second_grad = lax.psum_scatter(
        jnp.concatenate([up_down_grad, out_grad], 1), "col", scatter_dimension=0, tiled=True
    )
    second_grad = add_other_dp(second_grad)

    heads = block // HD
    delta = jnp.sum(
        (grad_att.astype(F32) * attended.astype(F32)).reshape(heads, HD, length), 1
    )
    delta = jnp.concatenate([delta, jnp.zeros((8 - heads, length), F32)], 0)
    grad_joint = jnp.concatenate(
        attend_backward(queries, keys, key_rows, value_rows, grad_att, lse, delta, labels), 0
    )
    grad_a = contract(w_joint, grad_joint, 1, 0)
    scaled_a = grad_a * gain_one
    sums = jnp.concatenate(
        [
            jnp.sum(scaled_a, 0, keepdims=True),
            jnp.sum(scaled_a * hat_a, 0, keepdims=True),
            jnp.zeros((14, length), F32),
        ],
        0,
    ).astype(BF16)
    sent = jnp.concatenate(
        [
            grad_a.astype(BF16).reshape(cols, features, length),
            jnp.broadcast_to(sums[None], (cols,) + sums.shape),
        ],
        1,
    )
    got = lax.all_to_all(sent, "col", 0, 0, tiled=True)
    got = jnp.sum(got.reshape(seqs, group, features + 16, length).astype(F32), 1)
    got = jnp.transpose(got, (1, 0, 2)).reshape(features + 16, held)
    grad_in = got[:features]
    hat_cols = (tokens.astype(F32) - center_all) * inverse_all
    grad_tokens = hidden_cols.astype(F32) + inverse_all * (
        grad_in * ln1_gain.astype(F32)[:, None]
        - got[features : features + 1] / wide
        - hat_cols * (got[features + 1 : features + 2] / wide)
    )

    joint_grad = contract(normed_a, grad_joint, 1, 1).astype(BF16)
    joint_grad = lax.ppermute(joint_grad, ("row", "col"), mixed)
    joint_grad = lax.psum_scatter(joint_grad, "col", scatter_dimension=0, tiled=True)
    joint_grad = add_other_dp(joint_grad)

    bias_sums = jnp.sum(grad_joint.astype(F32), 1)
    up_sums = jnp.sum(grad_pre.astype(F32), 1)
    small = jnp.concatenate(
        [
            put_block(jnp.sum(grad_in * hat_cols, 1), c, cols),
            put_block(jnp.sum(grad_in, 1), c, cols),
            put_block(jnp.sum(cotangent.astype(F32), 1), c, cols),
            jnp.sum(branch.astype(F32), 1),
            jnp.sum(grad_b * hat_b, 1),
            jnp.sum(grad_b, 1),
            put_block(bias_sums[:block], head, rows),
            put_block(bias_sums[2 * block :], head, rows),
            put_block(up_sums[:hidden_block], r, rows)
            + put_block(up_sums[hidden_block:], r ^ 2, rows),
        ]
    )
    small = lax.psum(small, ("dp", "row", "col"))
    by_col = [own_block(small[n * wide : (n + 1) * wide], c, features, 0) for n in range(6)]
    tail = small[6 * wide :]
    total_heads = block * rows
    q_sum = own_block(tail[:total_heads], r, block, 0)
    v_sum = own_block(tail[total_heads : 2 * total_heads], r, block, 0)
    up_sum = own_block(tail[2 * total_heads :], r, hidden_block, 0)
    return (
        out,
        grad_tokens,
        by_col[0],
        by_col[1],
        joint_grad[:, :block],
        q_sum,
        joint_grad[:, block : 2 * block],
        joint_grad[:, 2 * block :],
        v_sum,
        jnp.transpose(second_grad[:, 2 * hidden_block :]),
        by_col[3],
        by_col[4],
        by_col[5],
        second_grad[:, :hidden_block],
        up_sum,
        second_grad[:, hidden_block : 2 * hidden_block],
        by_col[2],
    )


def solution(mesh):
    placed = (
        P("col", ("dp", "row")),
        P("dp", None),
        P("col"),
        P("col"),
        P("col", "row"),
        P("row"),
        P("col", "row"),
        P("col", "row"),
        P("row"),
        P("row", "col"),
        P("col"),
        P("col"),
        P("col"),
        P("col", "row"),
        P("row"),
        P("col", "row"),
        P("col"),
        P("col", ("dp", "row")),
    )
    return jax.shard_map(
        local,
        mesh=mesh,
        in_specs=placed,
        out_specs=(
            P("col", ("dp", "row")),
            P("col", ("dp", "row")),
            P("col"),
            P("col"),
            P("col", "row"),
            P("row"),
            P("col", "row"),
            P("col", "row"),
            P("row"),
            P("row", "col"),
            P("col"),
            P("col"),
            P("col"),
            P("col", "row"),
            P("row"),
            P("col", "row"),
            P("col"),
        ),
        check_vma=False,
    )
```

time: 2550 us -> 587 us (0.23)
  waiting for transfers between devices: 2000 us -> 241 us
  matrix products: 262 us -> 50.2 us
  other arithmetic: 126 us -> 34.4 us
  local copies, waits for them, and re-layouts: 19.9 us -> 68.4 us
  starting transfers between devices: 1.21 us -> 44.6 us
  Pallas kernels: 0 us -> 37.2 us
  loops' own time: 29.2 us -> 0 us
    reduce_scatter x8 -> x2, waiting for transfers between devices: 1430 us -> 22.9 us  [the longest x1 22.9 us: local(): lax.psum_scatter(jnp.concatenate([up_down_grad, out_grad], 1), 'col', sca...]
    all_gather x8 -> x3, waiting for transfers between devices: 566 us -> 86 us  [the longest x1 63 us: local(): x_all = lax.all_gather(tokens, 'col', axis=0, tiled=True)]
    dot_general x40 -> x12, matrix products: 262 us -> 50.2 us  [contract(): lax.dot_general(left, right, (((left_dim,), (right_dim,)), ((), ())), pre...]
    all_to_all x0 -> x6, waiting for transfers between devices: none -> 88.7 us  [the longest x1 52.7 us: local(): got = lax.all_to_all(sent, 'col', 0, 0, tiled=True)]
    convert_element_type x29 -> x5, other arithmetic: 59.4 us -> 3.72 us  [the longest x1 2.37 us: local(): up_down_grad = (mine + swap(other, 2).astype(F32)).astype(BF16)]
    psum x6 -> x1, blocking collectives: 95.6 us -> 48.6 us  [local(): small = lax.psum(small, ('dp', 'row', 'col'))]
    all_gather x0 -> x2, blocking collectives: none -> 39.5 us  [the longest x1 34.4 us: local(): first_all = lax.all_gather(first_pack, 'col', axis=0, tiled=True)]
    pallas_call x0 -> x2, Pallas kernels: none -> 37.2 us  [the longest x1 18.9 us: attend_backward(): pl.pallas_call(functools.partial(backward_kernel, heads), grid_spec=pltpu...]
  transfers between devices with their start and end apart: 17 -> 22, of which waited for: 16 -> 10; matrix products, arithmetic and copies ran while one was open for 9% -> 20% of each run, Pallas kernels for 0% -> 6%
where the time goes in v1:
time: 587 us; the launch traced here: 579 us
  waiting for transfers between devices  241 us (41%)
  blocking collectives  88.1 us (15%)
  local copies, waits for them, and re-layouts  68.4 us (12%)
  matrix products  50.2 us (9%)
  starting transfers between devices  44.6 us (8%)
  Pallas kernels  37.2 us (6%)
  other arithmetic  34.4 us (6%)
  between operations  15.4 us (3%)
    all_gather x1, waiting for transfers between devices, local(): x_all = lax.all_gather(tokens, 'col', axis=0, tiled=True)  63 us
    all_to_all x1, waiting for transfers between devices, local(): got = lax.all_to_all(sent, 'col', 0, 0, tiled=True)  52.7 us
    dot_general x12, matrix products, contract(): lax.dot_general(left, right, (((left_dim,), (right_dim,)), ((), ())), pre...  50.2 us
    psum x1, blocking collectives, local(): small = lax.psum(small, ('dp', 'row', 'col'))  48.6 us
    all_gather x1, blocking collectives, local(): first_all = lax.all_gather(first_pack, 'col', axis=0, tiled=True)  34.4 us
    unnamed x7, waiting for transfers between devices  29.9 us
    all_gather x1, waiting for transfers between devices, local(): second_all = lax.all_gather(second_pack, 'col', axis=0, tiled=True)  23.1 us
    reduce_scatter x1, waiting for transfers between devices, local(): lax.psum_scatter(jnp.concatenate([up_down_grad, out_grad], 1), 'col', sca...  22.9 us
  transfers between devices with their start and end apart: 22, of which 10 were waited for; matrix products, arithmetic and copies ran while one was open for 20% of the time, Pallas kernels for 6%

profile of v1, /device:TPU:0, one launch (start us, length us, event | category | flops | bytes accessed | tf_op | source)
XLA Modules:
  0.0 578.9 jit_solution(16080552916163639874)
XLA Ops:
  12.1 34.4 %all_gather.25 = bf16[768,582]{1,0:T(8,128)(2,1)S(1)} all-gather(bf16[192,582]{1,0:T(8,128)(2,1)S(1)} %concatenate.65), channel_id=1, replica_groups=mesh['dp'=2,'row'=4,'col'=4] {'col'}, dimensions={0}, use_global_device_ids=true | all-gather | bytes 1117440 | tf_op jit(solution)/shard_map/all_gather | solution.py:239
  49.4 5.2 all-gather.2
  56.4 23.1 %all-gather.9.cloned.1.call-done = bf16[768,1728]{1,0:T(8,128)(2,1)} async-done(((bf16[192,1728]{1,0:T(8,128)(2,1)}), bf16[768,1728]{1,0:T(8,128)(2,1)}) %all-gather.9.cloned.1.call-update) | async-done | bytes 2654224 | tf_op jit(solution)/shard_map/all_gather | solution.py:259
  81.3 63.0 %all-gather.7.cloned.1.call-done = bf16[768,2048]{1,0:T(8,128)(2,1)} async-done(((bf16[192,2048]{1,0:T(8,128)(2,1)}), bf16[768,2048]{1,0:T(8,128)(2,1)}) %all-gather.7.cloned.1.call-update) | async-done | bytes 3145744 | tf_op jit(solution)/shard_map/all_gather | solution.py:240
  148.0 3.4 add_convert_fusion
  156.5 18.2 %attend_forward.1 = (bf16[192,2048]{1,0:T(8,128)(2,1)S(1)}, f32[8,2048]{1,0:T(8,128)S(1)}) custom-call(s32[8]{0:T(128)S(1)} %get-tuple-element.173.first_ref, s32[1,2048]{1,0:T(1,128)S(1)} %constant_dynamic-slice_fusion.4.seg_row, s32[2048,1]{1,0:T(8,128)S(1)} %copy.129.seg_col, bf16[192,2048]{1,0:T(8,128)(2,1)S(1)} %copy-done.5, ...), custom_call_target="tpu_custom_call" | custom-call | flops 1610612736 | bytes 3145728 | tf_op jit(solution)/shard_map/attend_forward/pallas_call | solution.py:72
  175.7 4.2 all-to-all-start
  179.9 3.2 slice.256
  189.2 12.0 %all-to-all-done = bf16[192,4,512]{2,0,1:T(8,128)(2,1)} async-done(((bf16[192,4,512]{2,0,1:T(8,128)(2,1)}), bf16[192,4,512]{2,0,1:T(8,128)(2,1)}, u32[]{:S(2)}, u32[]{:S(2)}) %all-to-all-start) | async-done | bytes 786464 | tf_op jit(solution)/shard_map/all_to_all | solution.py:284
  201.2 4.4 all-to-all-start.2
  210.9 15.2 %all-to-all-done.2 = bf16[192,4,512]{2,0,1:T(8,128)(2,1)} async-done(((bf16[192,4,512]{2,0,1:T(8,128)(2,1)}), bf16[192,4,512]{2,0,1:T(8,128)(2,1)}, u32[]{:S(2)}, u32[]{:S(2)}) %all-to-all-start.2) | async-done | bytes 786464 | tf_op jit(solution)/shard_map/all_to_all | solution.py:285
  226.1 3.2 fusion.42
  230.9 6.5 %collective-permute-done.1 = bf16[768,1536]{1,0:T(8,128)(2,1)} collective-permute-done((bf16[768,1536]{1,0:T(8,128)(2,1)}, bf16[768,1536]{1,0:T(8,128)(2,1)}, u32[]{:S(2)}, u32[]{:S(2)}) %collective-permute-start.1) | collective-permute-done | bytes 2359328 | tf_op jit(solution)/shard_map/ppermute | solution.py:191
  239.1 4.3 fusion.25
  246.3 8.8 %convert_reduce_fusion.2 = (f32[1536]{0:T(1024)S(1)}, bf16[1536,1024]{0,1:T(8,128)(2,1)S(1)}) fusion(f32[1536,1024]{0,1:T(8,128)S(1)} %fusion.25, f32[1536]{0:T(1024)S(1)} %pad_maximum_fusion.20, bf16[768,512]{1,0:T(8,128)(2,1)} %collective-permute-done.4, bf16[768,512]{1,0:T(8,128)(2,1)} %bitcast.20, bf16[768,768]{1,0:T(8,128)(2,1)S(1)} %get-tuple-element.134, ...), kind=kOutput, calls=%fused_computation.20 | convolution fusion | flops 2459957760 | bytes 13381632 | tf_op jit(solution)/shard_map/dot_general | solution.py:20
  258.6 6.1 %fusion.28 = f32[768,1536]{1,0:T(8,128)} fusion(bf16[768,512]{1,0:T(8,128)(2,1)} %collective-permute-done.4, bf16[768,512]{1,0:T(8,128)(2,1)} %bitcast.20, f32[1536,1024]{0,1:T(8,128)S(1)} %fusion.25, f32[1536]{0:T(1024)S(1)} %pad_maximum_fusion.20), kind=kOutput, calls=%fused_computation.74 | convolution fusion | flops 2434793472 | bytes 12589056 | tf_op jit(solution)/shard_map/dot_general | solution.py:20
  270.9 4.8 all-to-all-start.4
  275.7 5.0 fusion.29
  280.7 3.5 slice.336
  300.9 5.5 all-to-all-start.1
  314.7 18.9 %attend_backward.1 = (bf16[192,2048]{1,0:T(8,128)(2,1)S(1)}, bf16[192,2048]{1,0:T(8,128)(2,1)S(1)}, bf16[192,2048]{1,0:T(8,128)(2,1)S(1)}) custom-call(s32[8]{0:T(128)S(1)} %get-tuple-element.172.last_ref, s32[1,2048]{1,0:T(1,128)S(1)} %constant_dynamic-slice_fusion.4.seg_row, s32[2048,1]{1,0:T(8,128)S(1)} %copy.129.seg_col, ...), custom_call_target="tpu_custom_call" | custom-call | flops 4026531840 | bytes 6291456 | tf_op jit(solution)/shard_map/attend_backward/pallas_call | solution.py:156
  335.5 3.2 convolution_convert_fusion.1
  338.7 8.2 %collective-permute-start.6 = (bf16[768,576]{0,1:T(8,128)(2,1)}, bf16[768,576]{0,1:T(8,128)(2,1)}, u32[]{:S(2)}, u32[]{:S(2)}) collective-permute-start(bf16[768,576]{0,1:T(8,128)(2,1)} %convolution_convert_fusion.1), channel_id=1, source_target_pairs={{0,0},{1,5},{2,10},{3,15},{4,4},{5,1},{6,14},{7,11},{8,8},{9,13},{... | collective-permute-start | bytes 2654216 | tf_op jit(solution)/shard_map/ppermute | solution.py:370
  346.9 4.2 all-to-all-start.3
  351.2 7.2 %multiply_reduce_fusion = (bf16[2048]{0:T(1024)(128)(2,1)S(1)}, bf16[2048]{0:T(1024)(128)(2,1)S(1)}, bf16[768,2048]{1,0:T(8,128)(2,1)}) fusion(f32[768]{0:T(1024)S(1)} %get-tuple-element.123, f32[2048]{0:T(1024)S(1)} %add_rsqrt_fusion, f32[2048]{0:T(1024)S(1)} %broadcast_multiply_fusion, bf16[768,2048]{1,0:T(8,128)(2,1)S(1)} %copy-done.11, ...), kind=kOutput, calls=%fused_computation.22 | convolution fusion | flops 1824518144 | bytes 9563136 | tf_op jit(solution)/shard_map/dot_general | solution.py:20
  363.0 8.8 %all-to-all-done.3 = bf16[4,192,512]{2,1,0:T(8,128)(2,1)} async-done(((bf16[4,192,512]{2,1,0:T(8,128)(2,1)}), bf16[4,192,512]{2,1,0:T(8,128)(2,1)}, u32[]{:S(2)}, u32[]{:S(2)}) %all-to-all-start.3) | async-done | bytes 786464 | tf_op jit(solution)/shard_map/all_to_all | solution.py:314
  371.8 4.7 all-to-all-start.5
  390.5 29.1 %reduce-scatter.10.cloned.1.call-done = bf16[192,576]{1,0:T(8,128)(2,1)} async-done(((bf16[768,576]{1,0:T(8,128)(2,1)}), bf16[192,576]{1,0:T(8,128)(2,1)}) %reduce-scatter.10.cloned.1.call-update) | async-done | bytes 221200
  422.7 6.5 %collective-permute-done.7 = bf16[192,576]{0,1:T(8,128)(2,1)S(1)} collective-permute-done((bf16[192,576]{0,1:T(8,128)(2,1)S(1)}, bf16[192,576]{0,1:T(8,128)(2,1)S(1)}, u32[]{:S(2)}, u32[]{:S(2)}) %collective-permute-start.7) | collective-permute-done | bytes 221216 | tf_op jit(solution)/shard_map/ppermute | solution.py:195
  431.7 52.7 %all-to-all-done.5 = bf16[4,208,2048]{2,1,0:T(8,128)(2,1)} async-done(((bf16[4,208,2048]{2,1,0:T(8,128)(2,1)}), bf16[4,208,2048]{2,1,0:T(8,128)(2,1)}, u32[]{:S(2)}, u32[]{:S(2)}) %all-to-all-start.5) | async-done | bytes 3407904 | tf_op jit(solution)/shard_map/all_to_all | solution.py:358
  489.9 22.9 %reduce-scatter.8.cloned.1.call-done = bf16[192,1728]{1,0:T(8,128)(2,1)} async-done(((bf16[768,1728]{1,0:T(8,128)(2,1)}), bf16[192,1728]{1,0:T(8,128)(2,1)}) %reduce-scatter.8.cloned.1.call-update) | async-done | bytes 663568 | tf_op jit(solution)/shard_map/reduce_scatter | solution.py:328
  514.3 48.6 %psum.7 = f32[9216]{0:T(1024)S(1)} all-reduce(f32[9216]{0:T(1024)S(1)} %constant_dynamic-update-slice_fusion.4), channel_id=1, replica_groups=mesh['dp'=2,'row'=4,'col'=4] {'dp','row','col'}, use_global_device_ids=true, to_apply=%region_20.21 | all-reduce | flops 9216 | bytes 73728 | tf_op jit(solution)/shard_map/psum | solution.py:390
  (253 shorter events, 114.6 us)
Async XLA Ops:
  7.2 41.5 %copy-start = (s32[4,2048]{1,0:T(4,128)S(1)}, s32[4,2048]{1,0:T(4,128)}, u32[]{:S(2)}) copy-start(s32[4,2048]{1,0:T(4,128)} %param.19) | copy-start | bytes 98308
  7.3 4.6 copy-start.27
  7.3 4.6 copy-start.28
  7.3 72.2 %all-gather.9.cloned.1.call-start = ((), (), s32[]{:S(2)}) async-start(), calls=%async_computation.10 | async-start | bytes 3440640 | tf_op jit(solution)/shard_map/all_gather | solution.py:259
  10.4 133.8 %all-gather.7.cloned.1.call-start = ((), (), s32[]{:S(2)}) async-start(), calls=%async_computation.9 | async-start | bytes 3932160 | tf_op jit(solution)/shard_map/all_gather | solution.py:240
  11.2 175.5 %all-gather.11.cloned.1.call-start = ((), (), s32[]{:S(2)}) async-start(), calls=%async_computation.13 | async-start | bytes 1966080 | tf_op jit(solution)/shard_map/all_gather | solution.py:268
  11.9 37.4 %copy-start.30 = (bf16[768]{0:T(1024)(128)(2,1)S(1)}, bf16[768]{0:T(1024)(128)(2,1)}, u32[]{:S(2)}) copy-start(bf16[768]{0:T(1024)(128)(2,1)} %param.32) | copy-start | bytes 4612
  11.9 37.4 %copy-start.38 = (bf16[192]{0:T(256)(128)(2,1)S(1)}, bf16[192]{0:T(256)(128)(2,1)}, u32[]{:S(2)}) copy-start(bf16[192]{0:T(256)(128)(2,1)} %param.23) | copy-start | bytes 1156
  11.9 37.4 %copy-start.39 = (bf16[192]{0:T(256)(128)(2,1)S(1)}, bf16[192]{0:T(256)(128)(2,1)}, u32[]{:S(2)}) copy-start(bf16[192]{0:T(256)(128)(2,1)} %param.26) | copy-start | bytes 1156
  47.1 100.9 %collective-permute-start = (bf16[768,576]{0,1:T(8,128)(2,1)S(1)}, bf16[768,576]{0,1:T(8,128)(2,1)}, u32[]{:S(2)}, u32[]{:S(2)}) collective-permute-start(bf16[768,576]{0,1:T(8,128)(2,1)S(1)} %copy.127), channel_id=1, source_target_pairs={{0,0},{1,5},{2,10},{3,15},{4,4},{5,1},{6,14},{7,11},{8,8},{9,13},{... | collective-permute-start | bytes 2654216 | tf_op jit(solution)/shard_map/ppermute | solution.py:241
  175.7 25.6 %all-to-all-start = ((bf16[192,4,512]{2,0,1:T(8,128)(2,1)}), bf16[192,4,512]{2,0,1:T(8,128)(2,1)}, u32[]{:S(2)}, u32[]{:S(2)}) async-start(bf16[192,4,512]{2,0,1:T(8,128)(2,1)} %bitcast.111), calls=%async_computation | async-start | bytes 1572864 | tf_op jit(solution)/shard_map/all_to_all | solution.py:284
  183.1 54.2 %collective-permute-start.1 = (bf16[768,1536]{1,0:T(8,128)(2,1)}, bf16[768,1536]{1,0:T(8,128)(2,1)}, u32[]{:S(2)}, u32[]{:S(2)}) collective-permute-start(bf16[768,1536]{1,0:T(8,128)(2,1)} %slice.256), channel_id=1, source_target_pairs={{0,8},{4,12},{8,0},{12,4},{1,9},{5,13},{9,1},{13,5},{2,10},{6,14},... | collective-permute-start | bytes 7077896 | tf_op jit(solution)/shard_map/ppermute | solution.py:191
  201.2 24.9 %all-to-all-start.2 = ((bf16[192,4,512]{2,0,1:T(8,128)(2,1)}), bf16[192,4,512]{2,0,1:T(8,128)(2,1)}, u32[]{:S(2)}, u32[]{:S(2)}) async-start(bf16[192,4,512]{2,0,1:T(8,128)(2,1)} %bitcast.109), calls=%async_computation.2 | async-start | bytes 1572864 | tf_op jit(solution)/shard_map/all_to_all | solution.py:285
  210.8 28.3 %collective-permute-start.2 = (bf16[768,512]{1,0:T(8,128)(2,1)}, bf16[768,512]{1,0:T(8,128)(2,1)}, u32[]{:S(2)}, u32[]{:S(2)}) collective-permute-start(bf16[768,512]{1,0:T(8,128)(2,1)} %add_convert_fusion.2), channel_id=1, source_target_pairs={{0,4},{4,0},{8,12},{12,8},{1,5},{5,1},{9,13},{13,9},{2,6},{6,2},{1... | collective-permute-start | bytes 2359304 | tf_op jit(solution)/shard_map/ppermute | solution.py:191
  226.1 20.1 %collective-permute-start.4 = (bf16[768,512]{1,0:T(8,128)(2,1)}, bf16[768,512]{1,0:T(8,128)(2,1)}, u32[]{:S(2)}, u32[]{:S(2)}) collective-permute-start(bf16[768,512]{1,0:T(8,128)(2,1)} %bitcast.20), channel_id=1, source_target_pairs={{0,4},{4,0},{8,12},{12,8},{1,5},{5,1},{9,13},{13,9},{2,6},{6,2},{1... | collective-permute-start | bytes 2359304 | tf_op jit(solution)/shard_map/ppermute | solution.py:191
  230.9 8.3 %copy-start.21 = (bf16[768,768]{1,0:T(8,128)(2,1)S(1)}, bf16[768,768]{1,0:T(8,128)(2,1)}, u32[]{:S(2)}) copy-start(bf16[768,768]{1,0:T(8,128)(2,1)} %get-tuple-element.129) | copy-start | bytes 3538948
  257.8 6.9 %collective-permute-start.5 = (bf16[768,512]{1,0:T(8,128)(2,1)S(1)}, bf16[768,512]{1,0:T(8,128)(2,1)S(1)}, u32[]{:S(2)}, u32[]{:S(2)}) collective-permute-start(bf16[768,512]{1,0:T(8,128)(2,1)S(1)} %slice.338), channel_id=1, source_target_pairs={{0,4},{4,0},{8,12},{12,8},{1,5},{5,1},{9,13},{13,9},{2,6},{6,2},{1... | collective-permute-start | bytes 2359304 | tf_op jit(solution)/shard_map/ppermute | solution.py:191
  258.0 6.7 %copy-start.8 = (f32[768,512]{1,0:T(8,128)S(1)}, f32[768,512]{1,0:T(8,128)}, u32[]{:S(2)}) copy-start(f32[768,512]{1,0:T(8,128)} %copy-done.7) | copy-start | bytes 4718596
  258.0 7.6 %collective-permute-start.3 = (bf16[768,512]{1,0:T(8,128)(2,1)S(1)}, bf16[768,512]{1,0:T(8,128)(2,1)S(1)}, u32[]{:S(2)}, u32[]{:S(2)}) collective-permute-start(bf16[768,512]{1,0:T(8,128)(2,1)S(1)} %slice.339), channel_id=1, source_target_pairs={{0,4},{4,0},{8,12},{12,8},{1,5},{5,1},{9,13},{13,9},{2,6},{6,2},{1... | collective-permute-start | bytes 2359304 | tf_op jit(solution)/shard_map/ppermute | solution.py:191
  270.9 29.9 %all-to-all-start.4 = ((bf16[4,192,512]{2,1,0:T(8,128)(2,1)}), bf16[4,192,512]{2,1,0:T(8,128)(2,1)S(1)}, u32[]{:S(2)}, u32[]{:S(2)}) async-start(bf16[4,192,512]{2,1,0:T(8,128)(2,1)} %bitcast.121), calls=%async_computation.4 | async-start | bytes 1572864 | tf_op jit(solution)/shard_map/all_to_all | solution.py:313
  275.7 105.7 %reduce-scatter.6.cloned.1.call-start = ((), (), s32[]{:S(2)}) async-start(), calls=%async_computation.11 | async-start | bytes 1966080 | tf_op jit(solution)/shard_map/reduce_scatter | solution.py:327
  285.9 90.7 %collective-permute-start.8 = (bf16[768,1536]{1,0:T(8,128)(2,1)}, bf16[768,1536]{1,0:T(8,128)(2,1)}, u32[]{:S(2)}, u32[]{:S(2)}) collective-permute-start(bf16[768,1536]{1,0:T(8,128)(2,1)} %pad_maximum_fusion.4), channel_id=1, source_target_pairs={{0,8},{4,12},{8,0},{12,4},{1,9},{5,13},{9,1},{13,5},{2,10},{6,14},... | collective-permute-start | bytes 7077896 | tf_op jit(solution)/shard_map/ppermute | solution.py:191
  300.9 5.5 copy-start.17
  300.9 46.1 %all-to-all-start.1 = ((bf16[4,192,512]{2,1,0:T(8,128)(2,1)}), bf16[4,192,512]{2,1,0:T(8,128)(2,1)}, u32[]{:S(2)}, u32[]{:S(2)}) async-start(bf16[4,192,512]{2,1,0:T(8,128)(2,1)} %bitcast.114), calls=%async_computation.1 | async-start | bytes 1572864 | tf_op jit(solution)/shard_map/all_to_all | solution.py:298
  335.5 15.7 %copy-start.11 = (bf16[768,2048]{1,0:T(8,128)(2,1)S(1)}, bf16[768,2048]{1,0:T(8,128)(2,1)}, u32[]{:S(2)}) copy-start(bf16[768,2048]{1,0:T(8,128)(2,1)} %all-gather.7.cloned.1.call-done) | copy-start | bytes 9437188
  338.7 19.8 %collective-permute-start.6 = (bf16[768,576]{0,1:T(8,128)(2,1)}, bf16[768,576]{0,1:T(8,128)(2,1)}, u32[]{:S(2)}, u32[]{:S(2)}) collective-permute-start(bf16[768,576]{0,1:T(8,128)(2,1)} %convolution_convert_fusion.1), channel_id=1, source_target_pairs={{0,0},{1,5},{2,10},{3,15},{4,4},{5,1},{6,14},{7,11},{8,8},{9,13},{... | collective-permute-start | bytes 2654216 | tf_op jit(solution)/shard_map/ppermute | solution.py:370
  346.9 24.9 %all-to-all-start.3 = ((bf16[4,192,512]{2,1,0:T(8,128)(2,1)}), bf16[4,192,512]{2,1,0:T(8,128)(2,1)}, u32[]{:S(2)}, u32[]{:S(2)}) async-start(bf16[4,192,512]{2,1,0:T(8,128)(2,1)} %bitcast.113), calls=%async_computation.3 | async-start | bytes 1572864 | tf_op jit(solution)/shard_map/all_to_all | solution.py:314
  351.1 68.5 %reduce-scatter.10.cloned.1.call-start = ((), (), s32[]{:S(2)}) async-start(), calls=%async_computation.14 | async-start | bytes 1228800
  371.8 112.5 %all-to-all-start.5 = ((bf16[4,208,2048]{2,1,0:T(8,128)(2,1)}), bf16[4,208,2048]{2,1,0:T(8,128)(2,1)}, u32[]{:S(2)}, u32[]{:S(2)}) async-start(bf16[4,208,2048]{2,1,0:T(8,128)(2,1)} %pad_maximum_fusion), calls=%async_computation.5 | async-start | bytes 6815744 | tf_op jit(solution)/shard_map/all_to_all | solution.py:358
  376.6 136.2 %reduce-scatter.8.cloned.1.call-start = ((), (), s32[]{:S(2)}) async-start(), calls=%async_computation.12 | async-start | bytes 3440640 | tf_op jit(solution)/shard_map/reduce_scatter | solution.py:328
  420.8 8.4 %collective-permute-start.7 = (bf16[192,576]{0,1:T(8,128)(2,1)S(1)}, bf16[192,576]{0,1:T(8,128)(2,1)S(1)}, u32[]{:S(2)}, u32[]{:S(2)}) collective-permute-start(bf16[192,576]{0,1:T(8,128)(2,1)S(1)} %copy.146), channel_id=1, source_target_pairs={{0,16},{16,0},{1,17},{17,1},{2,18},{18,2},{3,19},{19,3},{4,20},{20... | collective-permute-start | bytes 663560 | tf_op jit(solution)/shard_map/ppermute | solution.py:195
  512.8 55.9 %collective-permute-start.9 = (bf16[192,1728]{1,0:T(8,128)(2,1)}, bf16[192,1728]{1,0:T(8,128)(2,1)S(1)}, u32[]{:S(2)}, u32[]{:S(2)}) collective-permute-start(bf16[192,1728]{1,0:T(8,128)(2,1)} %reduce-scatter.8.cloned.1.call-done), channel_id=1, source_target_pairs={{0,16},{16,0},{1,17},{17,1},{2,18},{18,2},{3,19},{19,3},{4,20},{20... | collective-permute-start | bytes 1990664 | tf_op jit(solution)/shard_map/ppermute | solution.py:195
  (33 other events, 90.8 us)
Sparse Core Ops, SparseCore 0:
  10.5 68.8 all-gather.8
  81.0 63.1 all-gather.6
  146.4 18.3 all-gather.10
  301.0 37.2 reduce-scatter.5
  361.0 58.5 reduce-scatter.9
  421.8 90.8 reduce-scatter.7

commit v2 on v1

--- a/solution.py
+++ b/solution.py
@@ -92,7 +92,7 @@
         ],
         compiler_params=pltpu.CompilerParams(vmem_limit_bytes=40 * 2**20),
         cost_estimate=pl.CostEstimate(
-            flops=2 * width * length * length, bytes_accessed=4 * 2 * width * length,
+            flops=24 * width * length * length, bytes_accessed=4 * 2 * width * length,
             transcendentals=heads * length * length // 2,
         ),
         name="attend_forward",
@@ -175,7 +175,7 @@
         out_shape=[jax.ShapeDtypeStruct((width, length), BF16)] * 3,
         compiler_params=pltpu.CompilerParams(vmem_limit_bytes=40 * 2**20),
         cost_estimate=pl.CostEstimate(
-            flops=5 * width * length * length, bytes_accessed=8 * 2 * width * length,
+            flops=28 * width * length * length, bytes_accessed=8 * 2 * width * length,
             transcendentals=heads * length * length // 2,
         ),
         name="attend_backward",
@@ -191,8 +191,26 @@
     return lax.ppermute(array, "row", [(place, place ^ bit) for place in range(count)])
 
 
-def add_other_dp(array):
-    return array.astype(F32) + lax.ppermute(array, "dp", [(0, 1), (1, 0)]).astype(F32)
+def cross_dp(array):
+    return lax.ppermute(array, "dp", [(0, 1), (1, 0)])
+
+
+def half_pair(array, side):
+    width = array.shape[1] // 2
+    low, high = array[:, :width], array[:, width:]
+    return jnp.where(side == 0, low, high), jnp.where(side == 0, high, low)
+
+
+def halve_dp(array, side):
+    kept, given = half_pair(array, side)
+    return kept + cross_dp(given.astype(BF16)).astype(F32)
+
+
+def join_dp(array, side):
+    other = cross_dp(array)
+    low = jnp.where(side == 0, array, other)
+    high = jnp.where(side == 0, other, array)
+    return jnp.concatenate([low, high], 1).astype(F32)
 
 
 def norm_stats(values):
@@ -256,6 +274,7 @@
         ]
     )
     second_pack = jnp.concatenate([w_up, w_down, jnp.transpose(w_out)], 1)
+    second_pack, x_all = lax.optimization_barrier((second_pack, x_all))
     second_all = lax.all_gather(second_pack, "col", axis=0, tiled=True)
     up_down = second_all[:, : 2 * hidden_block]
     up_down_other = swap(up_down, 2)
@@ -315,20 +334,27 @@
 
     down_grad = contract(ct_pair, activated, 1, 1)
     up_grad = contract(norm_pair, grad_pre, 1, 1)
-    other = jnp.concatenate(
-        [up_grad[:, hidden_block:].astype(BF16), down_grad[:, hidden_block:].astype(BF16)], 1
-    )
-    mine = jnp.concatenate([up_grad[:, :hidden_block], down_grad[:, :hidden_block]], 1)
-    up_down_grad = (mine + swap(other, 2).astype(F32)).astype(BF16)
+    side = lax.axis_index("dp")
+    kept_own, given_own = half_pair(up_grad[:, :hidden_block], side)
+    kept_far, given_far = half_pair(up_grad[:, hidden_block:], side)
+    given = cross_dp(jnp.concatenate([given_own, given_far], 1).astype(BF16)).astype(F32)
+    half = hidden_block // 2
+    up_far = swap((kept_far + given[:, half:]).astype(BF16), 2).astype(F32)
+    up_half = (kept_own + given[:, :half] + up_far).astype(BF16)
+    down_far = swap(down_grad[:, hidden_block:].astype(BF16), 2).astype(F32)
+    down_half = halve_dp(down_grad[:, :hidden_block] + down_far, side).astype(BF16)
     out_grad = contract(branch, att, 1, 1).astype(BF16)
-    out_grad = jnp.stack(
-        [own_block(out_grad, r ^ h, block, 1) for h in range(rows)], 0
-    )
-    out_grad = lax.psum_scatter(out_grad, "row", scatter_dimension=0, tiled=False)
+    out_grad = jnp.stack([own_block(out_grad, r ^ h, block, 1) for h in range(rows)], 0)
+    out_grad = lax.all_to_all(out_grad, "row", 0, 0, tiled=True)
+    out_grad, grad_att = lax.optimization_barrier((out_grad, grad_att))
+    out_grad = jnp.sum(out_grad.astype(F32), 0).astype(BF16)
+    out_grad = (out_grad.astype(F32) + cross_dp(out_grad).astype(F32)).astype(BF16)
     second_grad = lax.psum_scatter(
-        jnp.concatenate([up_down_grad, out_grad], 1), "col", scatter_dimension=0, tiled=True
-    )
-    second_grad = add_other_dp(second_grad)
+        jnp.concatenate([up_half, down_half, out_grad], 1), "col", scatter_dimension=0, tiled=True
+    )
+    grad_w_up = join_dp(second_grad[:, :half], side)
+    grad_w_down = join_dp(second_grad[:, half : 2 * half], side)
+    grad_w_out = jnp.transpose(second_grad[:, 2 * half :].astype(F32))
 
     heads = block // HD
     delta = jnp.sum(
@@ -366,17 +392,17 @@
         - hat_cols * (got[features + 1 : features + 2] / wide)
     )
 
-    joint_grad = contract(normed_a, grad_joint, 1, 1).astype(BF16)
+    joint_grad = halve_dp(contract(normed_a, grad_joint, 1, 1), side).astype(BF16)
     joint_grad = lax.ppermute(joint_grad, ("row", "col"), mixed)
     joint_grad = lax.psum_scatter(joint_grad, "col", scatter_dimension=0, tiled=True)
-    joint_grad = add_other_dp(joint_grad)
+    joint_grad = join_dp(joint_grad, side)
 
     bias_sums = jnp.sum(grad_joint.astype(F32), 1)
     up_sums = jnp.sum(grad_pre.astype(F32), 1)
     small = jnp.concatenate(
         [
-            put_block(jnp.sum(grad_in * hat_cols, 1), c, cols),
-            put_block(jnp.sum(grad_in, 1), c, cols),
+            jnp.sum(grad_a * hat_a, 1),
+            jnp.sum(grad_a, 1),
             put_block(jnp.sum(cotangent.astype(F32), 1), c, cols),
             jnp.sum(branch.astype(F32), 1),
             jnp.sum(grad_b * hat_b, 1),
@@ -404,13 +430,13 @@
         joint_grad[:, block : 2 * block],
         joint_grad[:, 2 * block :],
         v_sum,
-        jnp.transpose(second_grad[:, 2 * hidden_block :]),
+        grad_w_out,
         by_col[3],
         by_col[4],
         by_col[5],
-        second_grad[:, :hidden_block],
+        grad_w_up,
         up_sum,
-        second_grad[:, hidden_block : 2 * hidden_block],
+        grad_w_down,
         by_col[2],
     )
 

time: 587 us -> 558 us (0.951)
  waiting for transfers between devices: 241 us -> 128 us
  blocking collectives: 88.1 us -> 160 us
  other arithmetic: 34.4 us -> 47.3 us
  local copies, waits for them, and re-layouts: 68.4 us -> 55.8 us
  starting transfers between devices: 44.6 us -> 57 us
    psum x1, blocking collectives: 48.6 us -> 118 us  [local(): small = lax.psum(small, ('dp', 'row', 'col'))]
    all_to_all x1, waiting for transfers between devices: 52.7 us -> 0.01 us  [local(): got = lax.all_to_all(sent, 'col', 0, 0, tiled=True)]
    all_gather x1, waiting for transfers between devices: 63 us -> 33.4 us  [local(): x_all = lax.all_gather(tokens, 'col', axis=0, tiled=True)]
    unnamed x7 -> x6, waiting for transfers between devices: 29.9 us -> 0.77 us
    reduce_scatter x2 -> x1, waiting for transfers between devices: 22.9 us -> 0.02 us  [local(): lax.psum_scatter(jnp.concatenate([up_half, down_half, out_grad], 1), 'col...]
    all_gather x1, waiting for transfers between devices: 23.1 us -> 40.8 us  [local(): second_all = lax.all_gather(second_pack, 'col', axis=0, tiled=True)]
    convert_element_type x1 -> x11, other arithmetic: 2.37 us -> 13.9 us  [the longest x1 3.55 us: local(): up_far = swap((kept_far + given[:, half:]).astype(BF16), 2).astype(F32)]
    all_to_all x1, starting transfers between devices: 4.75 us -> 13.8 us  [local(): got = lax.all_to_all(sent, 'col', 0, 0, tiled=True)]
  transfers between devices with their start and end apart: 22 -> 28, of which waited for: 10 -> 9; matrix products, arithmetic and copies ran while one was open for 20% -> 22% of each run, Pallas kernels for 6% -> 7%
where the time goes in v2:
time: 558 us; the launch traced here: 550 us
  blocking collectives  160 us (29%)
  waiting for transfers between devices  128 us (23%)
  starting transfers between devices  57 us (10%)
  local copies, waits for them, and re-layouts  55.8 us (10%)
  matrix products  48.1 us (9%)
  other arithmetic  47.3 us (8%)
  Pallas kernels  39 us (7%)
  between operations  15.1 us (3%)
    psum x1, blocking collectives, local(): small = lax.psum(small, ('dp', 'row', 'col'))  118 us
    dot_general x12, matrix products, contract(): lax.dot_general(left, right, (((left_dim,), (right_dim,)), ((), ())), pre...  48.1 us
    all_gather x1, waiting for transfers between devices, local(): second_all = lax.all_gather(second_pack, 'col', axis=0, tiled=True)  40.8 us
    all_gather x1, blocking collectives, local(): first_all = lax.all_gather(first_pack, 'col', axis=0, tiled=True)  36.9 us
    all_gather x1, waiting for transfers between devices, local(): x_all = lax.all_gather(tokens, 'col', axis=0, tiled=True)  33.4 us
    pallas_call x1, Pallas kernels, attend_backward(): pl.pallas_call(functools.partial(backward_kernel, heads), grid_spec=pltpu...  19.9 us
    pallas_call x1, Pallas kernels, attend_forward(): pl.pallas_call(functools.partial(forward_kernel, heads), grid_spec=pltpu....  19.2 us
    unnamed x106, local copies, waits for them, and re-layouts  17.1 us
  transfers between devices with their start and end apart: 28, of which 9 were waited for; matrix products, arithmetic and copies ran while one was open for 22% of the time, Pallas kernels for 7%

profile of v2, /device:TPU:0, one launch (start us, length us, event | category | flops | bytes accessed | tf_op | source)
XLA Modules:
  0.0 550.3 jit_solution(10151389843380909434)
XLA Ops:
  13.8 36.9 %all_gather.25 = bf16[768,582]{1,0:T(8,128)(2,1)S(1)} all-gather(bf16[192,582]{1,0:T(8,128)(2,1)S(1)} %concatenate.72), channel_id=1, replica_groups=mesh['dp'=2,'row'=4,'col'=4] {'col'}, dimensions={0}, use_global_device_ids=true | all-gather | bytes 1117440 | tf_op jit(solution)/shard_map/all_gather | solution.py:257
  54.1 33.4 %all-gather.7.cloned.1.call-done = bf16[768,2048]{1,0:T(8,128)(2,1)} async-done(((bf16[192,2048]{1,0:T(8,128)(2,1)}), bf16[768,2048]{1,0:T(8,128)(2,1)}) %all-gather.7.cloned.1.call-update) | async-done | bytes 3145744 | tf_op jit(solution)/shard_map/all_gather | solution.py:258
  88.2 5.2 all-gather.2
  98.7 3.4 add_convert_fusion
  104.7 40.8 %all-gather.9.cloned.1.call-done = bf16[768,1728]{1,0:T(8,128)(2,1)} async-done(((bf16[192,1728]{1,0:T(8,128)(2,1)}), bf16[768,1728]{1,0:T(8,128)(2,1)}) %all-gather.9.cloned.1.call-update) | async-done | bytes 2654224 | tf_op jit(solution)/shard_map/all_gather | solution.py:278
  149.9 19.2 %attend_forward.1 = (bf16[192,2048]{1,0:T(8,128)(2,1)S(1)}, f32[8,2048]{1,0:T(8,128)S(1)}) custom-call(s32[8]{0:T(128)S(1)} %get-tuple-element.188.first_ref, s32[1,2048]{1,0:T(1,128)S(1)} %constant_dynamic-slice_fusion.seg_row, s32[2048,1]{1,0:T(8,128)S(1)} %copy.117.seg_col, bf16[192,2048]{1,0:T(8,128)(2,1)S(1)} %copy-done.5, ...), custom_call_target="tpu_custom_call" | custom-call | flops 19327352832 | bytes 3145728 | tf_op jit(solution)/shard_map/attend_forward/pallas_call | solution.py:72
  170.1 4.2 all-to-all-start
  174.3 3.3 slice.293
  185.0 9.7 %all-to-all-done = bf16[192,4,512]{2,0,1:T(8,128)(2,1)} async-done(((bf16[192,4,512]{2,0,1:T(8,128)(2,1)}), bf16[192,4,512]{2,0,1:T(8,128)(2,1)}, u32[]{:S(2)}, u32[]{:S(2)}) %all-to-all-start) | async-done | bytes 786464 | tf_op jit(solution)/shard_map/all_to_all | solution.py:303
  194.7 4.4 all-to-all-start.2
  205.5 13.2 %all-to-all-done.2 = bf16[192,4,512]{2,0,1:T(8,128)(2,1)} async-done(((bf16[192,4,512]{2,0,1:T(8,128)(2,1)}), bf16[192,4,512]{2,0,1:T(8,128)(2,1)}, u32[]{:S(2)}, u32[]{:S(2)}) %all-to-all-start.2) | async-done | bytes 786464 | tf_op jit(solution)/shard_map/all_to_all | solution.py:304
  222.1 8.7 %collective-permute-done.1 = bf16[768,1536]{1,0:T(8,128)(2,1)} collective-permute-done((bf16[768,1536]{1,0:T(8,128)(2,1)}, bf16[768,1536]{1,0:T(8,128)(2,1)}, u32[]{:S(2)}, u32[]{:S(2)}) %collective-permute-start.1) | collective-permute-done | bytes 2359328 | tf_op jit(solution)/shard_map/ppermute | solution.py:191
  232.6 4.2 fusion.26
  236.8 2.8 fusion.28
  239.6 8.8 %convert_reduce_fusion.2 = (f32[1536]{0:T(1024)S(1)}, bf16[1536,1024]{0,1:T(8,128)(2,1)S(1)}) fusion(f32[1536,1024]{0,1:T(8,128)S(1)} %fusion.26, f32[1536]{0:T(1024)S(1)} %pad_maximum_fusion.20, bf16[768,512]{1,0:T(8,128)(2,1)} %collective-permute-done.4, bf16[768,512]{1,0:T(8,128)(2,1)} %bitcast.20, bf16[768,768]{1,0:T(8,128)(2,1)S(1)} %get-tuple-element.144, ...), kind=kOutput, calls=%fused_computation.22 | convolution fusion | flops 2459957760 | bytes 13381632 | tf_op jit(solution)/shard_map/dot_general | solution.py:20
  252.0 4.2 fusion.32
  259.8 3.0 convert_reduce_fusion.4
  265.1 4.8 all-to-all-start.5
  269.8 5.0 fusion.33
  282.0 8.0 %all-to-all-done.5 = bf16[4,192,512]{2,1,0:T(8,128)(2,1)S(1)} async-done(((bf16[4,192,512]{2,1,0:T(8,128)(2,1)}), bf16[4,192,512]{2,1,0:T(8,128)(2,1)S(1)}, u32[]{:S(2)}, u32[]{:S(2)}) %all-to-all-start.5) | async-done | bytes 786464 | tf_op jit(solution)/shard_map/all_to_all | solution.py:332
  290.0 4.3 all-to-all-start.4
  298.9 7.6 %collective-permute-done.9 = bf16[768,768]{1,0:T(8,128)(2,1)} collective-permute-done((bf16[768,768]{1,0:T(8,128)(2,1)}, bf16[768,768]{1,0:T(8,128)(2,1)}, u32[]{:S(2)}, u32[]{:S(2)}) %collective-permute-start.9) | collective-permute-done | bytes 1179680 | tf_op jit(solution)/shard_map/ppermute | solution.py:195
  308.0 3.6 fusion.29
  313.0 5.5 %all-to-all-start.1 = ((bf16[4,192,512]{2,1,0:T(8,128)(2,1)}), bf16[4,192,512]{2,1,0:T(8,128)(2,1)}, u32[]{:S(2)}, u32[]{:S(2)}) async-start(bf16[4,192,512]{2,1,0:T(8,128)(2,1)} %bitcast.115), calls=%async_computation.1 | async-start | bytes 1572864 | tf_op jit(solution)/shard_map/all_to_all | solution.py:317
  325.4 19.9 %attend_backward.1 = (bf16[192,2048]{1,0:T(8,128)(2,1)S(1)}, bf16[192,2048]{1,0:T(8,128)(2,1)S(1)}, bf16[192,2048]{1,0:T(8,128)(2,1)S(1)}) custom-call(s32[8]{0:T(128)S(1)} %get-tuple-element.187.last_ref, s32[1,2048]{1,0:T(1,128)S(1)} %constant_dynamic-slice_fusion.seg_row, s32[2048,1]{1,0:T(8,128)S(1)} %copy.117.seg_col, ...), custom_call_target="tpu_custom_call" | custom-call | flops 22548578304 | bytes 6291456 | tf_op jit(solution)/shard_map/attend_backward/pallas_call | solution.py:156
  352.4 5.1 all-to-all-start.3
  357.5 7.9 %fusion.8 = (f32[768]{0:T(1024)S(1)}, bf16[2048]{0:T(1024)(128)(2,1)S(1)}, bf16[2048]{0:T(1024)(128)(2,1)S(1)}, f32[768]{0:T(1024)S(1)}, bf16[768,2048]{1,0:T(8,128)(2,1)}) fusion(bf16[768,2048]{1,0:T(8,128)(2,1)S(1)} %copy-done.13, f32[2048]{0:T(1024)S(1)} %add_rsqrt_fusion, f32[2048]{0:T(1024)S(1)} %broadcast_multiply_fusion, ...), kind=kOutput, calls=%fused_computation.13 | convolution fusion | flops 1829235200 | bytes 9569280 | tf_op jit(solution)/shard_map/dot_general | solution.py:20
  369.9 4.1 pad_maximum_fusion
  375.1 13.8 %all-to-all-start.6 = ((bf16[4,208,2048]{2,1,0:T(8,128)(2,1)}), bf16[4,208,2048]{2,1,0:T(8,128)(2,1)}, u32[]{:S(2)}, u32[]{:S(2)}) async-start(bf16[4,208,2048]{2,1,0:T(8,128)(2,1)} %pad_maximum_fusion), calls=%async_computation.6 | async-start | bytes 6815744 | tf_op jit(solution)/shard_map/all_to_all | solution.py:384
  396.2 117.7 %psum.7 = f32[9216]{0:T(1024)S(1)} all-reduce(f32[9216]{0:T(1024)S(1)} %constant_dynamic-update-slice_fusion.4), channel_id=1, replica_groups=mesh['dp'=2,'row'=4,'col'=4] {'dp','row','col'}, use_global_device_ids=true, to_apply=%region_20.21 | all-reduce | flops 9216 | bytes 73728 | tf_op jit(solution)/shard_map/psum | solution.py:416
  534.9 3.2 collective-permute-done.14
  539.0 2.8 convert_reduce_fusion.1
  (271 shorter events, 116.6 us)
Async XLA Ops:
  7.2 80.3 %copy-start = (s32[4,2048]{1,0:T(4,128)S(1)}, s32[4,2048]{1,0:T(4,128)}, u32[]{:S(2)}) copy-start(s32[4,2048]{1,0:T(4,128)} %param.19) | copy-start | bytes 98308
  7.2 45.8 %copy-start.33 = (bf16[192,192]{1,0:T(8,128)(2,1)S(1)}, bf16[192,192]{1,0:T(8,128)(2,1)}, u32[]{:S(2)}) copy-start(bf16[192,192]{1,0:T(8,128)(2,1)} %param.27) | copy-start | bytes 221188
  7.2 80.2 %all-gather.7.cloned.1.call-start = ((), (), s32[]{:S(2)}) async-start(), calls=%async_computation.9 | async-start | bytes 3932160 | tf_op jit(solution)/shard_map/all_gather | solution.py:258
  8.0 45.2 %copy-start.31 = (bf16[192,768]{1,0:T(8,128)(2,1)S(1)}, bf16[192,768]{1,0:T(8,128)(2,1)}, u32[]{:S(2)}) copy-start(bf16[192,768]{1,0:T(8,128)(2,1)} %param.33) | copy-start | bytes 884740
  8.0 45.2 %copy-start.32 = (bf16[192,768]{1,0:T(8,128)(2,1)S(1)}, bf16[192,768]{1,0:T(8,128)(2,1)}, u32[]{:S(2)}) copy-start(bf16[192,768]{1,0:T(8,128)(2,1)} %param.31) | copy-start | bytes 884740
  8.0 137.6 %all-gather.9.cloned.1.call-start = ((), (), s32[]{:S(2)}) async-start(), calls=%async_computation.10 | async-start | bytes 3440640 | tf_op jit(solution)/shard_map/all_gather | solution.py:278
  51.3 47.4 %collective-permute-start = (bf16[768,576]{0,1:T(8,128)(2,1)S(1)}, bf16[768,576]{0,1:T(8,128)(2,1)}, u32[]{:S(2)}, u32[]{:S(2)}) collective-permute-start(bf16[768,576]{0,1:T(8,128)(2,1)S(1)} %copy.115), channel_id=1, source_target_pairs={{0,0},{1,5},{2,10},{3,15},{4,4},{5,1},{6,14},{7,11},{8,8},{9,13},{... | collective-permute-start | bytes 2654216 | tf_op jit(solution)/shard_map/ppermute | solution.py:259
  87.4 95.0 %all-gather.11.cloned.1.call-start = ((), (), s32[]{:S(2)}) async-start(), calls=%async_computation.12 | async-start | bytes 1966080 | tf_op jit(solution)/shard_map/all_gather | solution.py:287
  170.1 24.6 %all-to-all-start = ((bf16[192,4,512]{2,0,1:T(8,128)(2,1)}), bf16[192,4,512]{2,0,1:T(8,128)(2,1)}, u32[]{:S(2)}, u32[]{:S(2)}) async-start(bf16[192,4,512]{2,0,1:T(8,128)(2,1)} %bitcast.112), calls=%async_computation | async-start | bytes 1572864 | tf_op jit(solution)/shard_map/all_to_all | solution.py:303
  177.5 53.3 %collective-permute-start.1 = (bf16[768,1536]{1,0:T(8,128)(2,1)}, bf16[768,1536]{1,0:T(8,128)(2,1)}, u32[]{:S(2)}, u32[]{:S(2)}) collective-permute-start(bf16[768,1536]{1,0:T(8,128)(2,1)} %slice.293), channel_id=1, source_target_pairs={{0,8},{4,12},{8,0},{12,4},{1,9},{5,13},{9,1},{13,5},{2,10},{6,14},... | collective-permute-start | bytes 7077896 | tf_op jit(solution)/shard_map/ppermute | solution.py:191
  194.7 24.1 %all-to-all-start.2 = ((bf16[192,4,512]{2,0,1:T(8,128)(2,1)}), bf16[192,4,512]{2,0,1:T(8,128)(2,1)}, u32[]{:S(2)}, u32[]{:S(2)}) async-start(bf16[192,4,512]{2,0,1:T(8,128)(2,1)} %bitcast.110), calls=%async_computation.2 | async-start | bytes 1572864 | tf_op jit(solution)/shard_map/all_to_all | solution.py:304
  204.2 28.4 %collective-permute-start.2 = (bf16[768,512]{1,0:T(8,128)(2,1)}, bf16[768,512]{1,0:T(8,128)(2,1)}, u32[]{:S(2)}, u32[]{:S(2)}) collective-permute-start(bf16[768,512]{1,0:T(8,128)(2,1)} %add_convert_fusion.2), channel_id=1, source_target_pairs={{0,4},{4,0},{8,12},{12,8},{1,5},{5,1},{9,13},{13,9},{2,6},{6,2},{1... | collective-permute-start | bytes 2359304 | tf_op jit(solution)/shard_map/ppermute | solution.py:191
  218.8 20.9 %collective-permute-start.4 = (bf16[768,512]{1,0:T(8,128)(2,1)}, bf16[768,512]{1,0:T(8,128)(2,1)}, u32[]{:S(2)}, u32[]{:S(2)}) collective-permute-start(bf16[768,512]{1,0:T(8,128)(2,1)} %bitcast.20), channel_id=1, source_target_pairs={{0,4},{4,0},{8,12},{12,8},{1,5},{5,1},{9,13},{13,9},{2,6},{6,2},{1... | collective-permute-start | bytes 2359304 | tf_op jit(solution)/shard_map/ppermute | solution.py:191
  251.2 7.6 %collective-permute-start.5 = (bf16[768,512]{1,0:T(8,128)(2,1)S(1)}, bf16[768,512]{1,0:T(8,128)(2,1)S(1)}, u32[]{:S(2)}, u32[]{:S(2)}) collective-permute-start(bf16[768,512]{1,0:T(8,128)(2,1)S(1)} %slice.418), channel_id=1, source_target_pairs={{0,4},{4,0},{8,12},{12,8},{1,5},{5,1},{9,13},{13,9},{2,6},{6,2},{1... | collective-permute-start | bytes 2359304 | tf_op jit(solution)/shard_map/ppermute | solution.py:191
  251.4 8.3 %collective-permute-start.3 = (bf16[768,512]{1,0:T(8,128)(2,1)S(1)}, bf16[768,512]{1,0:T(8,128)(2,1)S(1)}, u32[]{:S(2)}, u32[]{:S(2)}) collective-permute-start(bf16[768,512]{1,0:T(8,128)(2,1)S(1)} %slice.419), channel_id=1, source_target_pairs={{0,4},{4,0},{8,12},{12,8},{1,5},{5,1},{9,13},{13,9},{2,6},{6,2},{1... | collective-permute-start | bytes 2359304 | tf_op jit(solution)/shard_map/ppermute | solution.py:191
  257.4 36.9 %collective-permute-start.11 = (bf16[768,768]{1,0:T(8,128)(2,1)}, bf16[768,768]{1,0:T(8,128)(2,1)}, u32[]{:S(2)}, u32[]{:S(2)}) collective-permute-start(bf16[768,768]{1,0:T(8,128)(2,1)} %slice.417), channel_id=1, source_target_pairs={{0,8},{4,12},{8,0},{12,4},{1,9},{5,13},{9,1},{13,5},{2,10},{6,14},... | collective-permute-start | bytes 3538952 | tf_op jit(solution)/shard_map/ppermute | solution.py:191
  265.1 24.9 %all-to-all-start.5 = ((bf16[4,192,512]{2,1,0:T(8,128)(2,1)}), bf16[4,192,512]{2,1,0:T(8,128)(2,1)S(1)}, u32[]{:S(2)}, u32[]{:S(2)}) async-start(bf16[4,192,512]{2,1,0:T(8,128)(2,1)} %bitcast.118), calls=%async_computation.5 | async-start | bytes 1572864 | tf_op jit(solution)/shard_map/all_to_all | solution.py:332
  277.3 29.2 %collective-permute-start.9 = (bf16[768,768]{1,0:T(8,128)(2,1)}, bf16[768,768]{1,0:T(8,128)(2,1)}, u32[]{:S(2)}, u32[]{:S(2)}) collective-permute-start(bf16[768,768]{1,0:T(8,128)(2,1)} %pad_maximum_fusion.14), channel_id=1, source_target_pairs={{0,16},{16,0},{1,17},{17,1},{2,18},{18,2},{3,19},{19,3},{4,20},{20... | collective-permute-start | bytes 3538952 | tf_op jit(solution)/shard_map/ppermute | solution.py:195
  290.0 22.9 %all-to-all-start.4 = ((bf16[4,768,192]{1,2,0:T(8,128)(2,1)}), bf16[4,768,192]{1,2,0:T(8,128)(2,1)}, u32[]{:S(2)}, u32[]{:S(2)}) async-start(bf16[4,768,192]{1,2,0:T(8,128)(2,1)} %pad_maximum_fusion.13), calls=%async_computation.4 | async-start | bytes 2359296 | tf_op jit(solution)/shard_map/all_to_all | solution.py:348
  297.6 93.9 %collective-permute-start.12 = (bf16[768,384]{1,0:T(8,128)(2,1)}, bf16[768,384]{1,0:T(8,128)(2,1)}, u32[]{:S(2)}, u32[]{:S(2)}) collective-permute-start(bf16[768,384]{1,0:T(8,128)(2,1)} %select_convert_fusion), channel_id=1, source_target_pairs={{0,16},{16,0},{1,17},{17,1},{2,18},{18,2},{3,19},{19,3},{4,20},{20... | collective-permute-start | bytes 1769480 | tf_op jit(solution)/shard_map/ppermute | solution.py:195
  311.5 77.4 %collective-permute-start.10 = (bf16[768,384]{1,0:T(8,128)(2,1)}, bf16[768,384]{1,0:T(8,128)(2,1)}, u32[]{:S(2)}, u32[]{:S(2)}) collective-permute-start(bf16[768,384]{1,0:T(8,128)(2,1)} %fusion.29), channel_id=1, source_target_pairs={{0,8},{4,12},{8,0},{12,4},{1,9},{5,13},{9,1},{13,5},{2,10},{6,14},... | collective-permute-start | bytes 1769480 | tf_op jit(solution)/shard_map/ppermute | solution.py:191
  313.0 39.4 %all-to-all-start.1 = ((bf16[4,192,512]{2,1,0:T(8,128)(2,1)}), bf16[4,192,512]{2,1,0:T(8,128)(2,1)}, u32[]{:S(2)}, u32[]{:S(2)}) async-start(bf16[4,192,512]{2,1,0:T(8,128)(2,1)} %bitcast.115), calls=%async_computation.1 | async-start | bytes 1572864 | tf_op jit(solution)/shard_map/all_to_all | solution.py:317
  350.9 17.0 %collective-permute-start.6 = (bf16[768,288]{0,1:T(8,128)(2,1)}, bf16[768,288]{0,1:T(8,128)(2,1)}, u32[]{:S(2)}, u32[]{:S(2)}) collective-permute-start(bf16[768,288]{0,1:T(8,128)(2,1)} %select_convert_fusion.3), channel_id=1, source_target_pairs={{0,16},{16,0},{1,17},{17,1},{2,18},{18,2},{3,19},{19,3},{4,20},{20... | collective-permute-start | bytes 1327112 | tf_op jit(solution)/shard_map/ppermute | solution.py:195
  352.4 22.7 %all-to-all-start.3 = ((bf16[4,192,512]{2,1,0:T(8,128)(2,1)}), bf16[4,192,512]{2,1,0:T(8,128)(2,1)}, u32[]{:S(2)}, u32[]{:S(2)}) async-start(bf16[4,192,512]{2,1,0:T(8,128)(2,1)} %bitcast.114), calls=%async_computation.3 | async-start | bytes 1572864 | tf_op jit(solution)/shard_map/all_to_all | solution.py:333
  357.5 157.7 %reduce-scatter.7.cloned.1.call-start = ((), (), s32[]{:S(2)}) async-start(), calls=%async_computation.13 | async-start | bytes 737280
  367.3 25.8 %collective-permute-start.13 = (bf16[768,192]{1,0:T(8,128)(2,1)S(1)}, bf16[768,192]{1,0:T(8,128)(2,1)S(1)}, u32[]{:S(2)}, u32[]{:S(2)}) collective-permute-start(bf16[768,192]{1,0:T(8,128)(2,1)S(1)} %copy.125), channel_id=1, source_target_pairs={{0,16},{16,0},{1,17},{17,1},{2,18},{18,2},{3,19},{19,3},{4,20},{20... | collective-permute-start | bytes 884744 | tf_op jit(solution)/shard_map/ppermute | solution.py:195
  369.1 4.9 collective-permute-start.7
  375.1 163.9 %all-to-all-start.6 = ((bf16[4,208,2048]{2,1,0:T(8,128)(2,1)}), bf16[4,208,2048]{2,1,0:T(8,128)(2,1)}, u32[]{:S(2)}, u32[]{:S(2)}) async-start(bf16[4,208,2048]{2,1,0:T(8,128)(2,1)} %pad_maximum_fusion), calls=%async_computation.6 | async-start | bytes 6815744 | tf_op jit(solution)/shard_map/all_to_all | solution.py:384
  388.9 137.8 %reduce-scatter.5.cloned.1.call-start = ((), (), s32[]{:S(2)}) async-start(), calls=%async_computation.11 | async-start | bytes 1966080 | tf_op jit(solution)/shard_map/reduce_scatter | solution.py:352
  516.3 10.3 %collective-permute-start.8 = (bf16[192,288]{0,1:T(8,128)(2,1)S(1)}, bf16[192,288]{0,1:T(8,128)(2,1)S(1)}, u32[]{:S(2)}, u32[]{:S(2)}) collective-permute-start(bf16[192,288]{0,1:T(8,128)(2,1)S(1)} %copy.132), channel_id=1, source_target_pairs={{0,16},{16,0},{1,17},{17,1},{2,18},{18,2},{3,19},{19,3},{4,20},{20... | collective-permute-start | bytes 331784 | tf_op jit(solution)/shard_map/ppermute | solution.py:195
  527.7 5.2 collective-permute-start.15
  532.9 5.2 collective-permute-start.14
  (40 other events, 232.2 us)
Sparse Core Ops, SparseCore 0:
  9.6 77.7 all-gather.6
  89.0 56.5 all-gather.8
  147.7 18.3 all-gather.10
  375.2 50.8 reduce-scatter.6
  428.8 72.4 reduce-scatter.4
